TPU v7x, 256 devices: a whole 4x4x8 slice. The times are simulated.
256 devices in a mesh: prow: 8 (over y, core), pcol: 32 (over x, z).
Axes of the slice: x: 4, y: 4, z: 8, core: 2. Of those that a mesh axis runs over, the one named last changes fastest.
Arguments:
- trailing: float32 [16384, 16384], P('prow', 'pcol'), as said below
- panel: float32 [16384, 256], P('prow', 'pcol'), as said below
Outputs:
- updated: float32 [16384, 16384], P('prow', 'pcol')
- work_matrix: float32 [16384, 256], P('prow', 'pcol')
Inputs may be any that keep to these rules, and one draw needn't show every extreme that they name: trailing equals its transpose. panel has full column rank.
All inputs are finite; a program needn't handle non-finite values.
Results may differ from a plain program's by a relative error of at most 0.00016.
Values sent between devices are 32-bit elements; how exact they have to be, the bound alone decides.
A program may use at most 128 MiB of HBM per device.

v0:
```python
import functools

import jax
import jax.numpy as jnp
from jax import lax
from jax.experimental import pallas as pl
from jax.experimental.pallas import tpu as pltpu
from jax.sharding import PartitionSpec as P

HIGH = lax.Precision.HIGHEST
F32 = jnp.float32
NX, NZ, NY = 4, 8, 4
VMEM = pl.BlockSpec(memory_space=pltpu.VMEM)
ANY = pl.BlockSpec(memory_space=pl.ANY)
LIMIT = 48 << 20
NN, NT, TN = ((1,), (0,)), ((1,), (1,)), ((0,), (0,))


def mm(a, b, dims=NN):
    return lax.dot_general(a, b, (dims, ((), ())), precision=HIGH, preferred_element_type=F32)


def split(x):
    hi = x.astype(jnp.bfloat16)
    return hi, (x - hi.astype(F32)).astype(jnp.bfloat16)


def mm3(a, b, dims=NN):
    (ah, al), (bh, bl) = a, b

    def dot(l, r):
        return lax.dot_general(l, r, (dims, ((), ())), preferred_element_type=F32)

    return dot(ah, bh) + (dot(ah, bl) + dot(al, bh))


def iota(shape, dim):
    return lax.broadcasted_iota(jnp.int32, shape, dim)


BASE = 64


def base_inverse(block):
    n = BASE
    row = iota((8, 128), 0)
    eye = (iota((n, n), 0) == iota((n, n), 1)).astype(F32)
    x = jnp.concatenate([block, eye], axis=1)
    groups = [x[8 * g : 8 * g + 8, :] for g in range(n // 8)]
    zero = jnp.zeros((8, 128), F32)

    def column(vals):
        v = zero
        for i, e in enumerate(vals):
            if e is not None:
                v = jnp.where(row == i, e, v)
        return v

    out = []
    for k in range(n // 8):
        gk = groups[k]
        rows = [jnp.broadcast_to(gk[m : m + 1, :], (8, 128)) for m in range(8)]
        a = [[None] * 8 for _ in range(8)]
        for i in range(8):
            for j in range(i + 1):
                a[i][j] = jnp.broadcast_to(rows[j][:, 8 * k + i : 8 * k + i + 1], (8, 128))
        acols = {
            g: [jnp.broadcast_to(groups[g][:, 8 * k + m : 8 * k + m + 1], (8, 128)) for m in range(8)]
            for g in range(k + 1, n // 8)
        }
        l = [[None] * 8 for _ in range(8)]
        r = [None] * 8
        for j in range(8):
            r[j] = lax.rsqrt(a[j][j])
            for i in range(j + 1, 8):
                l[i][j] = a[i][j] * r[j]
            for i in range(j + 1, 8):
                for c in range(j + 1, i + 1):
                    a[i][c] = a[i][c] - l[i][j] * l[c][j]
        w = [[None] * 8 for _ in range(8)]
        for j in range(8):
            w[j][j] = r[j]
            for i in range(j + 1, 8):
                s = l[i][j] * w[j][j]
                for c in range(j + 1, i):
                    s = s + l[i][c] * w[c][j]
                w[i][j] = -(s * r[i])
        cols = [column([w[i][m] for i in range(8)]) for m in range(8)]
        u = cols[0] * rows[0]
        for m in range(1, 8):
            u = u + cols[m] * rows[m]
        out.append(u)
        if k + 1 < n // 8:
            cols_t = [column([w[j][m] for m in range(8)]) for j in range(8)]
            z = cols_t[0] * jnp.broadcast_to(u[0:1, :], (8, 128))
            for j in range(1, 8):
                z = z + cols_t[j] * jnp.broadcast_to(u[j : j + 1, :], (8, 128))
            z_rows = [jnp.broadcast_to(z[m : m + 1, :], (8, 128)) for m in range(8)]
            for g in range(k + 1, n // 8):
                s = acols[g][0] * z_rows[0]
                for m in range(1, 8):
                    s = s + acols[g][m] * z_rows[m]
                groups[g] = groups[g] - s
    inv = jnp.concatenate(out, axis=0)[:, n:]
    return jnp.where(iota((n, n), 1) <= iota((n, n), 0), inv, 0.0)


def lower_inverse(gram):
    size = gram.shape[0]
    if size == BASE:
        return base_inverse(gram)
    h = size // 2
    i_top = lower_inverse(gram[:h, :h])
    l_side = mm(gram[h:, :h], i_top, NT)
    i_bot = lower_inverse(gram[h:, h:] - mm(l_side, l_side, NT))
    i_side = -mm(i_bot, mm(l_side, i_top))
    top = jnp.concatenate([i_top, jnp.zeros((h, h), F32)], 1)
    return jnp.concatenate([top, jnp.concatenate([i_side, i_bot], 1)], 0)


def upper_inverse(y):
    n = y.shape[0]
    r, c = iota((n, n), 0), iota((n, n), 1)
    inv = jnp.where(r == c, 1.0 / y, 0.0)
    s = 1
    while s < n:
        off = (r // (2 * s) == c // (2 * s)) & (r // s != c // s) & (r < c)
        inv = inv - mm(inv, mm(jnp.where(off, y, 0.0), inv))
        s *= 2
    return inv


def meet(peers):
    barrier = pltpu.get_barrier_semaphore()
    for peer in peers:
        pl.semaphore_signal(barrier, inc=1, device_id=peer, device_id_type=pl.DeviceIdType.MESH)
    pl.semaphore_wait(barrier, len(peers))


def remote(src, dst, send, recv, peer):
    return pltpu.make_async_remote_copy(
        src_ref=src, dst_ref=dst, send_sem=send, recv_sem=recv, device_id=peer, device_id_type=pl.DeviceIdType.MESH
    )


def place():
    prow, pcol = lax.axis_index("prow"), lax.axis_index("pcol")
    return prow // 2, prow % 2, pcol // NZ, pcol % NZ


def gather_peers():
    _, _, x, z = place()
    peers = [{"pcol": x * NZ + (z + 1) % NZ}, {"pcol": x * NZ + (z + NZ - 1) % NZ}]
    return peers + [{"pcol": (x + dx) % NX * NZ + z} for dx in range(1, NX)]


def gather(rows, out, send, recv):
    _, core, x, z = place()

    def slab(xx, zz):
        start = (xx % NX * NZ + (zz + 2 * NZ) % NZ) * rows
        return out.at[pl.ds(pl.multiple_of(start, rows), rows)]

    def along_z(dx, dist):
        step = 1 if dist <= NZ // 2 else -1
        piece = slab(x + dx, z + step - dist)
        return remote(piece, piece, send.at[dx, dist], recv.at[dx, dist], {"pcol": x * NZ + (z + step + NZ) % NZ})

    def along_x(dx, dist):
        piece = slab(x, z - dist)
        return remote(piece, piece, send.at[dx, dist], recv.at[dx, dist], {"pcol": (x + NX - dx) % NX * NZ + z})

    def arrived(dx, dist):
        piece = slab(x + dx, z - dist)
        remote(piece, piece, send.at[dx, dist], recv.at[dx, dist], {"pcol": x * NZ + (z + 1) % NZ}).wait_recv()

    def passed_on(dx, dist):
        if dist < NZ // 2:
            along_z(dx, dist + 1).start()
        elif dist > NZ // 2 + 1:
            along_z(dx, dist - 1).start()

    order = (1, 7, 2, 6, 3, 5, 4)

    @pl.when(core == 0)
    def _():
        along_z(0, 1).start()
        along_z(0, NZ - 1).start()
        for dx in range(1, NX):
            along_x(dx, 0).start()
        for dist in order:
            arrived(0, dist)
            passed_on(0, dist)
            for dx in range(1, NX):
                along_x(dx, dist).start()
        for dist in (0,) + order:
            for dx in range(1, NX):
                arrived(dx, dist)

    @pl.when(core == 1)
    def _():
        for dx in range(1, NX):
            along_x(dx, 0).start()
        along_z(0, 1).start()
        along_z(0, NZ - 1).start()
        for dx in range(1, NX):
            arrived(dx, 0)
            along_z(dx, 1).start()
            along_z(dx, NZ - 1).start()
        for dist in order:
            for dx in range(NX):
                arrived(dx, dist)
                passed_on(dx, dist)

    for dx in range(NX):
        for dist in range(NZ):
            if dx or dist:
                piece = slab(x, z)
                remote(piece, piece, send.at[dx, dist], recv.at[dx, dist], {"pcol": x * NZ + (z + 1) % NZ}).wait_send()


def column_peers():
    y, core, _, _ = place()
    peers = [{"prow": (y + dy) % NY * 2 + core} for dy in range(1, NY)]
    return peers + [{"prow": y * 2 + 1 - core}]


class Broadcast:
    def __init__(self, y0, core0, src, out, send, recv):
        y, core, _, _ = place()
        self.owner = (y == y0) & (core == core0)
        self.relay = (y != y0) & (core == core0)
        self.leaf = core != core0
        self.along = [
            remote(src, out, send.at[dy], recv.at[0], {"prow": (y + dy) % NY * 2 + core}) for dy in range(1, NY)
        ]
        self.own = remote(src, out, send.at[0], recv.at[0], {"prow": y * 2 + 1 - core})
        self.pass_on = remote(out, out, send.at[0], recv.at[0], {"prow": y * 2 + 1 - core})
        self.keep = pltpu.make_async_copy(src, out, send.at[NY])

    def start(self):
        @pl.when(self.owner)
        def _():
            for copy in self.along:
                copy.start()
            self.own.start()
            self.keep.start()

    def finish(self):
        @pl.when(self.relay)
        def _():
            self.pass_on.wait_recv()
            self.pass_on.start()
            self.pass_on.wait_send()

        @pl.when(self.leaf)
        def _():
            self.pass_on.wait_recv()

        @pl.when(self.owner)
        def _():
            for copy in self.along:
                copy.wait_send()
            self.own.wait_send()
            self.keep.wait()


def panel_kernel(slab_ref, a_ref, out_ref, top_ref, send, recv, tsend, trecv):
    _, _, x, z = place()
    rows = slab_ref.shape[0]
    out_ref[pl.ds(pl.multiple_of((x * NZ + z) * rows, rows), rows), :] = slab_ref[...]
    meet(gather_peers() + column_peers())
    top = Broadcast(0, 0, a_ref.at[pl.ds(0, top_ref.shape[0])], top_ref, tsend, trecv)
    top.start()
    gather(rows, out_ref, send, recv)
    top.finish()


def rows_kernel(xc_ref, pt_ref, out_ref, pc_ref, first, send, recv, psend, precv, fsem):
    y, core, x, z = place()
    prow, pcol = y * 2 + core, x * NZ + z
    rows = first.shape[0]
    cols = pc_ref.shape[1]
    mine = xc_ref.at[pl.ds(pl.multiple_of(prow * rows, rows), rows)]
    to_row, to_col = pcol // 4, pcol % 4 * 8 + prow
    from_col, from_row = prow * 4 + pcol // 8, pcol % 8
    stays = (to_row == prow) & (to_col == pcol)
    target = {"prow": to_row, "pcol": to_col}
    source = {"prow": from_row, "pcol": from_col}

    barrier = pltpu.get_barrier_semaphore()
    peers = gather_peers() + column_peers()
    for peer in peers:
        pl.semaphore_signal(barrier, inc=1, device_id=peer, device_id_type=pl.DeviceIdType.MESH)

    @pl.when(jnp.logical_not(stays))
    def _():
        pl.semaphore_signal(barrier, inc=1, device_id=target, device_id_type=pl.DeviceIdType.MESH)
        pl.semaphore_signal(barrier, inc=1, device_id=source, device_id_type=pl.DeviceIdType.MESH)
        pl.semaphore_wait(barrier, len(peers) + 2)

    @pl.when(stays)
    def _():
        pl.semaphore_wait(barrier, len(peers))

    out_own = pl.ds(pl.multiple_of(pcol * rows, rows), rows)
    swap = remote(mine, first, fsem.at[0], fsem.at[1], target)

    @pl.when(jnp.logical_not(stays))
    def _():
        swap.start()

    offset = pl.multiple_of(pcol % 4 * cols, cols)
    part = Broadcast(x, z // 4, pt_ref.at[:, pl.ds(offset, cols)], pc_ref, psend, precv)
    part.start()

    @pl.when(jnp.logical_not(stays))
    def _():
        swap.wait_recv()
        out_ref[out_own, :] = first[...]

    @pl.when(stays)
    def _():
        out_ref[out_own, :] = xc_ref[pl.ds(pl.multiple_of(prow * rows, rows), rows), :]

    gather(rows, out_ref, send, recv)
    part.finish()

    @pl.when(jnp.logical_not(stays))
    def _():
        swap.wait_send()


def reduce_kernel(extra, *refs):
    if extra:
        s_ref, e_ref, out_ref, half, quarter, acc, send, recv, esend, erecv = refs
    else:
        s_ref, out_ref, half, quarter, acc, send, recv = refs
        e_ref = esend = erecv = None
    y, core, _, _ = place()
    prow = y * 2 + core
    width = s_ref.shape[1]
    q = s_ref.shape[0] // 8
    h = 4 * q
    mate = {"prow": y * 2 + 1 - core}

    def along(dy):
        return {"prow": (y + dy) % NY * 2 + core}

    meet([{"prow": (prow + d) % 8} for d in range(1, 8)])

    def rows(start, n):
        return pl.ds(pl.multiple_of(start, n), n)

    own = rows(core * h + y * q, q)
    exchange = remote(s_ref.at[rows((1 - core) * h, h)], half, send.at[0], recv.at[0], mate)
    exchange.start()
    handed = []
    if extra:
        for r in range(1, 8):
            piece = pl.ds(r % 2 * h + r // 2 * q, q)
            handed.append(
                remote(
                    e_ref.at[piece, pl.ds(0, extra)],
                    out_ref.at[piece, pl.ds(width, extra)],
                    esend.at[r],
                    erecv.at[0],
                    {"prow": r},
                )
            )

        @pl.when(prow == 0)
        def _():
            for copy in handed:
                copy.start()
            out_ref[pl.ds(0, q), pl.ds(width, extra)] = e_ref[pl.ds(0, q), pl.ds(0, extra)]

    exchange.wait_recv()
    acc[...] = s_ref[rows(core * h, h), :] + half[...]
    quarters = []
    for dy in range(1, NY):
        to = (y + dy) % NY
        quarters.append(remote(acc.at[rows(to * q, q)], quarter.at[dy], send.at[dy], recv.at[dy], along(dy)))
        quarters[-1].start()
    total = acc[rows(y * q, q), :]
    for copy, dy in zip(quarters, range(1, NY)):
        copy.wait_recv()
        total = total + quarter[dy]
    out_ref[own, pl.ds(0, width)] = total
    if extra:

        @pl.when(prow != 0)
        def _():
            remote(e_ref.at[own, pl.ds(0, extra)], out_ref.at[own, pl.ds(width, extra)], esend.at[0], erecv.at[0], mate).wait_recv()

    done = []
    for dy in range(1, NY):
        done.append(remote(out_ref.at[own], out_ref.at[own], send.at[3 + dy], recv.at[3 + dy], along(dy)))
        done[-1].start()
    passed = [remote(out_ref.at[own], out_ref.at[own], send.at[7], recv.at[7], mate)]
    passed[0].start()
    for dy in range(1, NY):
        theirs = rows(core * h + (y + NY - dy) % NY * q, q)
        remote(out_ref.at[theirs], out_ref.at[theirs], send.at[3 + dy], recv.at[3 + dy], mate).wait_recv()
        passed.append(remote(out_ref.at[theirs], out_ref.at[theirs], send.at[7 + dy], recv.at[7 + dy], mate))
        passed[-1].start()
    for dy in range(NY):
        theirs = rows((1 - core) * h + (y + NY - dy) % NY * q, q)
        remote(out_ref.at[theirs], out_ref.at[theirs], send.at[7 + dy], recv.at[7 + dy], mate).wait_recv()
    for copy in [exchange] + quarters + done + passed:
        copy.wait_send()
    if extra:

        @pl.when(prow == 0)
        def _():
            for copy in handed:
                copy.wait_send()


def params(cid):
    return pltpu.CompilerParams(collective_id=cid, has_side_effects=True, vmem_limit_bytes=LIMIT)


def plain(**kw):
    return pltpu.CompilerParams(vmem_limit_bytes=LIMIT, **kw)


def shape(*dims):
    return jax.ShapeDtypeStruct(dims, F32)


def all_reduce(s, e, extra, cid):
    n, width = s.shape
    dma = pltpu.SemaphoreType.DMA
    scratch = [pltpu.VMEM((n // 2, width), F32), pltpu.VMEM((4, n // 8, width), F32), pltpu.VMEM((n // 2, width), F32)]
    scratch += [dma((11,)), dma((11,))]
    args = [s]
    if extra:
        args.append(e)
        scratch += [dma((8,)), dma((1,))]
    return pl.pallas_call(
        functools.partial(reduce_kernel, extra),
        out_shape=shape(n, width + extra),
        in_specs=[VMEM] * len(args),
        out_specs=VMEM,
        scratch_shapes=scratch,
        compiler_params=params(cid),
    )(*args)


def products_kernel(pt_ref, a_ref, s_ref):
    pt = pt_ref[...]
    nb = pt.shape[0]
    s_ref[:, 0:nb] = mm(pt, pt, NT)
    s_ref[:, nb:] = mm3(split(pt), split(a_ref[...]))


def factor_kernel(s_ref, ae_ref, linv_ref, t_ref, xct_ref, xc_ref):
    nb = s_ref.shape[0]
    cols = ae_ref.shape[1]
    linv = lower_inverse(s_ref[:, 0:nb])
    linv_ref[...] = linv
    side = mm(linv, s_ref[:, nb + cols :])
    r, c = iota((nb, nb), 0), iota((nb, nb), 1)
    eye = (r == c).astype(F32)
    ygram = 2.0 * eye - side - mm(s_ref[:, nb + cols :], linv, ((0,), (1,)))
    t = upper_inverse(jnp.where(r < c, ygram, jnp.where(r == c, 0.5 * ygram, 0.0)))
    t_ref[...] = t
    avt = mm(linv, s_ref[:, nb : nb + cols]) - ae_ref[...]
    xct = mm(t, avt, TN)
    xct_ref[...] = xct
    xc_ref[...] = xct.T


def project_kernel(pt_ref, xr_ref, linv_ref, m_ref):
    nb = pt_ref.shape[0]
    m = mm(linv_ref[...], mm3(split(pt_ref[...]), split(xr_ref[...])))
    first = lax.axis_index("prow") == 0
    m_ref[...] = m - jnp.where(first, xr_ref[0:nb, :], 0.0)


def update_kernel(a_ref, pt_ref, xr_ref, pct_ref, xct_ref, linv_ref, t_ref, m_ref, o_ref, w_ref, bh, bl, vh, vl, bt, kl):
    nb, cols = pct_ref.shape
    step = pl.program_id(0)
    prow, pcol = lax.axis_index("prow"), lax.axis_index("pcol")
    at_top = (prow == 0) & (step == 0)

    @pl.when(step == 0)
    def _():
        linv = linv_ref[...]
        vct = mm(linv, pct_ref[...])
        e = (iota((nb, cols), 0) == iota((nb, cols), 1)) & (pcol == 0)
        vct = vct - e.astype(F32)
        k = mm(t_ref[...], m_ref[...], TN)
        wct = xct_ref[...] - 0.5 * mm(k, vct, TN)
        b = wct - 0.5 * mm(k, vct)
        bt[...] = b
        bh[...], bl[...] = split(mm(linv, b, TN))
        vh[...], vl[...] = split(vct)
        sel = (iota((8, nb), 1) == iota((8, nb), 0) + 8 * pcol).astype(F32)
        kt = mm(sel, k, NT)
        kl[0:8, :] = kt
        kl[8:16, :] = mm(kt, linv)
        kl[16:24, :] = sel

    p, x = pt_ref[...], xr_ref[...]
    ps, xs = split(p), split(x)
    both = mm3(ps, (bh[...], bl[...]), TN) + mm3(xs, (vh[...], vl[...]))
    o_ref[...] = a_ref[...] - both
    w_ref[...] = mm(kl[16:24, :], x, NT) - 0.5 * mm(kl[8:16, :], p)

    @pl.when(at_top)
    def _():
        o_ref[...] += bt[...]
        w_ref[...] += 0.5 * kl[0:8, :]


def shards(trailing, panel):
    rows, cols = trailing.shape
    pt_own = panel.T
    nc = pt_own.shape[0]
    nb = nc * lax.axis_size("pcol")
    dma = pltpu.SemaphoreType.DMA

    pt, ae = pl.pallas_call(
        panel_kernel,
        out_shape=(shape(nb, rows), shape(nb, cols)),
        in_specs=[VMEM, ANY],
        out_specs=(VMEM, VMEM),
        scratch_shapes=[dma((NX, NZ)), dma((NX, NZ)), dma((NY + 1,)), dma((1,))],
        compiler_params=params(1),
    )(pt_own, trailing)

    s = pl.pallas_call(
        products_kernel,
        out_shape=shape(nb, nb + cols),
        in_specs=[VMEM, VMEM],
        out_specs=VMEM,
        compiler_params=plain(),
    )(pt, trailing)

    s = all_reduce(s, pt, nb, 2)

    linv, t, xct, xc = pl.pallas_call(
        factor_kernel,
        out_shape=(shape(nb, nb), shape(nb, nb), shape(nb, cols), shape(cols, nb)),
        in_specs=[VMEM, VMEM],
        out_specs=(VMEM,) * 4,
        compiler_params=plain(),
    )(s, ae)

    xr, pct = pl.pallas_call(
        rows_kernel,
        out_shape=(shape(rows, nb), shape(nb, cols)),
        in_specs=[VMEM, VMEM],
        out_specs=(VMEM, VMEM),
        scratch_shapes=[
            pltpu.VMEM((cols // 8, nb), F32),
            dma((NX, NZ)),
            dma((NX, NZ)),
            dma((NY + 1,)),
            dma((1,)),
            dma((2,)),
        ],
        compiler_params=params(3),
    )(xc, pt)

    m = pl.pallas_call(
        project_kernel,
        out_shape=shape(nb, nb),
        in_specs=[VMEM] * 3,
        out_specs=VMEM,
        compiler_params=plain(),
    )(pt, xr, linv)
    m = all_reduce(m, None, 0, 4)

    tile = nb
    whole = lambda *dims: pl.BlockSpec(dims, lambda i: (0, 0))
    updated, wt = pl.pallas_call(
        update_kernel,
        grid=(rows // tile,),
        out_shape=(shape(rows, cols), shape(nc, rows)),
        in_specs=[
            pl.BlockSpec((tile, cols), lambda i: (i, 0)),
            pl.BlockSpec((nb, tile), lambda i: (0, i)),
            pl.BlockSpec((tile, nb), lambda i: (i, 0)),
            whole(nb, cols),
            whole(nb, cols),
            whole(nb, nb),
            whole(nb, nb),
            whole(nb, nb),
        ],
        out_specs=(pl.BlockSpec((tile, cols), lambda i: (i, 0)), pl.BlockSpec((nc, tile), lambda i: (0, i))),
        scratch_shapes=[pltpu.VMEM((nb, cols), jnp.bfloat16)] * 4 + [pltpu.VMEM((nb, cols), F32), pltpu.VMEM((24, nb), F32)],
        compiler_params=plain(dimension_semantics=("arbitrary",)),
    )(trailing, pt, xr, pct, xct, linv, t, m)
    return updated, wt.T


def solution(mesh):
    in_specs = (P("prow", "pcol"), P("prow", "pcol"))
    out_specs = (P("prow", "pcol"), P("prow", "pcol"))
    return jax.shard_map(shards, mesh=mesh, in_specs=in_specs, out_specs=out_specs, check_vma=False)
```

profile of v0, /device:TPU:1, one launch (start us, length us, event | category | flops | bytes accessed | tf_op | source)
XLA Modules:
  0.0 141.1 jit_solution(7777473726287159783)
XLA Ops:
  0.6 0.0 copy-start
  0.6 0.8 copy-done
  1.5 28.9 %shard_map.41 = (f32[256,2048]{1,0:T(8,128)S(1)}, f32[256,512]{1,0:T(8,128)S(1)}) custom-call(f32[8,2048]{1,0:T(8,128)S(1)} %bitcast.2, f32[2048,512]{1,0:T(8,128)} %a_ref.5), custom_call_target="tpu_custom_call" | custom-call | tf_op jit(solution)/shard_map/pallas_call | solution.py:525
  30.4 5.6 %shard_map.42.refs_0_ = f32[256,768]{1,0:T(8,128)S(1)} custom-call(f32[256,2048]{1,0:T(8,128)S(1)} %get-tuple-element.12.pt_ref.refs_1_, f32[2048,512]{1,0:T(8,128)} %a_ref.5), custom_call_target="tpu_custom_call" | custom-call | tf_op jit(solution)/shard_map/pallas_call | solution.py:534
  36.0 23.1 %shard_map.43.s_ref = f32[256,1024]{1,0:T(8,128)S(1)} custom-call(f32[256,768]{1,0:T(8,128)S(1)} %shard_map.42.refs_0_, f32[256,2048]{1,0:T(8,128)S(1)} %get-tuple-element.12.pt_ref.refs_1_), custom_call_target="tpu_custom_call" | custom-call | tf_op jit(solution)/shard_map/pallas_call | solution.py:441
  59.1 21.9 %shard_map.44 = (f32[256,256]{1,0:T(8,128)S(1)}, f32[256,256]{1,0:T(8,128)S(1)}, f32[256,512]{1,0:T(8,128)S(1)}, f32[512,256]{1,0:T(8,128)S(1)}) custom-call(f32[256,1024]{1,0:T(8,128)S(1)} %shard_map.43.s_ref, f32[256,512]{1,0:T(8,128)S(1)} %get-tuple-element.13.ae_ref), custom_call_target="tpu_custom_call" | custom-call | tf_op jit(solution)/shard_map/pallas_call | solution.py:544
  81.0 27.8 %shard_map.45 = (f32[2048,256]{1,0:T(8,128)S(1)}, f32[256,512]{1,0:T(8,128)S(1)}) custom-call(f32[512,256]{1,0:T(8,128)S(1)} %get-tuple-element.14.xc_ref, f32[256,2048]{1,0:T(8,128)S(1)} %get-tuple-element.12.pt_ref.refs_1_), custom_call_target="tpu_custom_call" | custom-call | tf_op jit(solution)/shard_map/pallas_call | solution.py:552
  108.8 1.7 %shard_map.46.refs_0_ = f32[256,256]{1,0:T(8,128)S(1)} custom-call(f32[256,2048]{1,0:T(8,128)S(1)} %get-tuple-element.12.pt_ref.refs_1_, f32[2048,256]{1,0:T(8,128)S(1)} %get-tuple-element.15.xr_ref, f32[256,256]{1,0:T(8,128)S(1)} %get-tuple-element.18.linv_ref), custom_call_target="tpu_custom_call" | custom-call | tf_op jit(solution)/shard_map/pallas_call | solution.py:568
  110.5 17.1 %shard_map.47.m_ref = f32[256,256]{1,0:T(8,128)S(1)} custom-call(f32[256,256]{1,0:T(8,128)S(1)} %shard_map.46.refs_0_), custom_call_target="tpu_custom_call" | custom-call | tf_op jit(solution)/shard_map/pallas_call | solution.py:441
  127.7 13.4 %shard_map.48 = (f32[2048,512]{1,0:T(8,128)}, f32[8,2048]{1,0:T(8,128)}) custom-call(f32[2048,512]{1,0:T(8,128)} %a_ref.5, f32[256,2048]{1,0:T(8,128)S(1)} %get-tuple-element.12.pt_ref.refs_1_, f32[2048,256]{1,0:T(8,128)S(1)} %get-tuple-element.15.xr_ref, f32[256,512]{1,0:T(8,128)S(1)} %get-tuple-element.16.pct_ref, ...), custom_call_target="tpu_custom_call" | custom-call | tf_op jit(solution)/shard_map/pallas_call | solution.py:579
Async XLA Ops:
  0.6 0.8 copy-start
where the time goes:
time: 141 us
  Pallas kernels  140 us (99%)
    pallas_call x2, Pallas kernels, all_reduce(): pl.pallas_call(functools.partial(reduce_kernel, extra), out_shape=shape(n...  40.2 us
    pallas_call x1, Pallas kernels, shards(): pl.pallas_call(panel_kernel, out_shape=(shape(nb, rows), shape(nb, cols))...  28.9 us
    pallas_call x1, Pallas kernels, shards(): pl.pallas_call(rows_kernel, out_shape=(shape(rows, nb), shape(nb, cols)),...  27.8 us
    pallas_call x1, Pallas kernels, shards(): pl.pallas_call(factor_kernel, out_shape=(shape(nb, nb), shape(nb, nb), sh...  21.9 us
    pallas_call x1, Pallas kernels, shards(): pl.pallas_call(update_kernel, grid=(rows // tile,), out_shape=(shape(rows...  13.4 us
    pallas_call x1, Pallas kernels, shards(): pl.pallas_call(products_kernel, out_shape=shape(nb, nb + cols), in_specs=...  5.62 us

commit v1 on v0

v1 whole, which is shorter than its diff:
```python
import jax
import jax.numpy as jnp
from jax import lax
from jax.experimental import pallas as pl
from jax.experimental.pallas import tpu as pltpu
from jax.sharding import PartitionSpec as P

HIGH = lax.Precision.HIGHEST
F32 = jnp.float32
NX, NZ, NY = 4, 8, 4
VMEM = pl.BlockSpec(memory_space=pltpu.VMEM)
ANY = pl.BlockSpec(memory_space=pl.ANY)
LIMIT = 48 << 20
NN, NT, TN = ((1,), (0,)), ((1,), (1,)), ((0,), (0,))


def mm(a, b, dims=NN):
    return lax.dot_general(a, b, (dims, ((), ())), precision=HIGH, preferred_element_type=F32)


def split(x):
    hi = x.astype(jnp.bfloat16)
    return hi, (x - hi.astype(F32)).astype(jnp.bfloat16)


def mm3(a, b, dims=NN):
    (ah, al), (bh, bl) = a, b

    def dot(l, r):
        return lax.dot_general(l, r, (dims, ((), ())), preferred_element_type=F32)

    return dot(ah, bh) + (dot(ah, bl) + dot(al, bh))


def iota(shape, dim):
    return lax.broadcasted_iota(jnp.int32, shape, dim)


BASE = 64


def base_inverse(block):
    n = BASE
    row = iota((8, 128), 0)
    eye = (iota((n, n), 0) == iota((n, n), 1)).astype(F32)
    x = jnp.concatenate([block, eye], axis=1)
    groups = [x[8 * g : 8 * g + 8, :] for g in range(n // 8)]
    zero = jnp.zeros((8, 128), F32)

    def column(vals):
        v = zero
        for i, e in enumerate(vals):
            if e is not None:
                v = jnp.where(row == i, e, v)
        return v

    out = []
    for k in range(n // 8):
        gk = groups[k]
        rows = [jnp.broadcast_to(gk[m : m + 1, :], (8, 128)) for m in range(8)]
        a = [[None] * 8 for _ in range(8)]
        for i in range(8):
            for j in range(i + 1):
                a[i][j] = jnp.broadcast_to(rows[j][:, 8 * k + i : 8 * k + i + 1], (8, 128))
        acols = {
            g: [jnp.broadcast_to(groups[g][:, 8 * k + m : 8 * k + m + 1], (8, 128)) for m in range(8)]
            for g in range(k + 1, n // 8)
        }
        l = [[None] * 8 for _ in range(8)]
        r = [None] * 8
        for j in range(8):
            r[j] = lax.rsqrt(a[j][j])
            for i in range(j + 1, 8):
                l[i][j] = a[i][j] * r[j]
            for i in range(j + 1, 8):
                for c in range(j + 1, i + 1):
                    a[i][c] = a[i][c] - l[i][j] * l[c][j]
        w = [[None] * 8 for _ in range(8)]
        for j in range(8):
            w[j][j] = r[j]
            for i in range(j + 1, 8):
                s = l[i][j] * w[j][j]
                for c in range(j + 1, i):
                    s = s + l[i][c] * w[c][j]
                w[i][j] = -(s * r[i])
        cols = [column([w[i][m] for i in range(8)]) for m in range(8)]
        u = cols[0] * rows[0]
        for m in range(1, 8):
            u = u + cols[m] * rows[m]
        out.append(u)
        if k + 1 < n // 8:
            cols_t = [column([w[j][m] for m in range(8)]) for j in range(8)]
            z = cols_t[0] * jnp.broadcast_to(u[0:1, :], (8, 128))
            for j in range(1, 8):
                z = z + cols_t[j] * jnp.broadcast_to(u[j : j + 1, :], (8, 128))
            z_rows = [jnp.broadcast_to(z[m : m + 1, :], (8, 128)) for m in range(8)]
            for g in range(k + 1, n // 8):
                s = acols[g][0] * z_rows[0]
                for m in range(1, 8):
                    s = s + acols[g][m] * z_rows[m]
                groups[g] = groups[g] - s
    inv = jnp.concatenate(out, axis=0)[:, n:]
    return jnp.where(iota((n, n), 1) <= iota((n, n), 0), inv, 0.0)


def lower_inverse(gram, hook):
    size = gram.shape[0]
    if size == BASE:
        inv = base_inverse(gram)
        hook()
        return inv
    h = size // 2
    i_top = lower_inverse(gram[:h, :h], hook)
    l_side = mm(gram[h:, :h], i_top, NT)
    i_bot = lower_inverse(gram[h:, h:] - mm(l_side, l_side, NT), hook)
    i_side = -mm(i_bot, mm(l_side, i_top))
    top = jnp.concatenate([i_top, jnp.zeros((h, h), F32)], 1)
    return jnp.concatenate([top, jnp.concatenate([i_side, i_bot], 1)], 0)


def upper_base(y):
    n = y.shape[0]
    r, c = iota((n, n), 0), iota((n, n), 1)
    inv = jnp.where(r == c, 1.0 / y, 0.0)
    s = 1
    while s < n:
        off = (r // (2 * s) == c // (2 * s)) & (r // s != c // s) & (r < c)
        inv = inv - mm(inv, mm(jnp.where(off, y, 0.0), inv))
        s *= 2
    return inv


def upper_inverse(y):
    size = y.shape[0]
    if size == BASE:
        return upper_base(y)
    h = size // 2
    i_top = upper_inverse(y[:h, :h])
    i_bot = upper_inverse(y[h:, h:])
    i_side = -mm(i_top, mm(y[:h, h:], i_bot))
    bottom = jnp.concatenate([jnp.zeros((h, h), F32), i_bot], 1)
    return jnp.concatenate([jnp.concatenate([i_top, i_side], 1), bottom], 0)


def meet(peers):
    barrier = pltpu.get_barrier_semaphore()
    for peer in peers:
        pl.semaphore_signal(barrier, inc=1, device_id=peer, device_id_type=pl.DeviceIdType.MESH)
    pl.semaphore_wait(barrier, len(peers))


def remote(src, dst, send, recv, peer):
    return pltpu.make_async_remote_copy(
        src_ref=src, dst_ref=dst, send_sem=send, recv_sem=recv, device_id=peer, device_id_type=pl.DeviceIdType.MESH
    )


def place():
    prow, pcol = lax.axis_index("prow"), lax.axis_index("pcol")
    return prow // 2, prow % 2, pcol // NZ, pcol % NZ


def gather_peers():
    _, _, x, z = place()
    peers = [{"pcol": x * NZ + (z + 1) % NZ}, {"pcol": x * NZ + (z + NZ - 1) % NZ}]
    return peers + [{"pcol": (x + dx) % NX * NZ + z} for dx in range(1, NX)]


def gather(rows, out, send, recv, hooks=()):
    _, core, x, z = place()

    def slab(xx, zz):
        start = (xx % NX * NZ + (zz + 2 * NZ) % NZ) * rows
        return out.at[pl.ds(pl.multiple_of(start, rows), rows)]

    def along_z(dx, dist):
        step = 1 if dist <= NZ // 2 else -1
        piece = slab(x + dx, z + step - dist)
        return remote(piece, piece, send.at[dx, dist], recv.at[dx, dist], {"pcol": x * NZ + (z + step + NZ) % NZ})

    def along_x(dx, dist):
        piece = slab(x, z - dist)
        return remote(piece, piece, send.at[dx, dist], recv.at[dx, dist], {"pcol": (x + NX - dx) % NX * NZ + z})

    def arrived(dx, dist):
        piece = slab(x + dx, z - dist)
        remote(piece, piece, send.at[dx, dist], recv.at[dx, dist], {"pcol": x * NZ + (z + 1) % NZ}).wait_recv()

    def passed_on(dx, dist):
        if dist < NZ // 2:
            along_z(dx, dist + 1).start()
        elif dist > NZ // 2 + 1:
            along_z(dx, dist - 1).start()

    order = (1, 7, 2, 6, 3, 5, 4)

    @pl.when(core == 0)
    def _():
        along_z(0, 1).start()
        along_z(0, NZ - 1).start()
        for dx in range(1, NX):
            along_x(dx, 0).start()

    @pl.when(core == 1)
    def _():
        for dx in range(1, NX):
            along_x(dx, 0).start()
        along_z(0, 1).start()
        along_z(0, NZ - 1).start()
        for dx in range(1, NX):
            arrived(dx, 0)
            along_z(dx, 1).start()
            along_z(dx, NZ - 1).start()

    for i, dist in enumerate(order):

        @pl.when(core == 0)
        def _():
            arrived(0, dist)
            passed_on(0, dist)
            for dx in range(1, NX):
                along_x(dx, dist).start()

        @pl.when(core == 1)
        def _():
            for dx in range(NX):
                arrived(dx, dist)
                passed_on(dx, dist)

        if i < len(hooks):
            hooks[i]()

    @pl.when(core == 0)
    def _():
        for dist in (0,) + order:
            for dx in range(1, NX):
                arrived(dx, dist)

    for dx in range(NX):
        for dist in range(NZ):
            if dx or dist:
                piece = slab(x, z)
                remote(piece, piece, send.at[dx, dist], recv.at[dx, dist], {"pcol": x * NZ + (z + 1) % NZ}).wait_send()


def column_peers():
    y, core, _, _ = place()
    peers = [{"prow": (y + dy) % NY * 2 + core} for dy in range(1, NY)]
    return peers + [{"prow": y * 2 + 1 - core}]


class Broadcast:
    def __init__(self, y0, core0, src, out, send, recv):
        y, core, _, _ = place()
        self.owner = (y == y0) & (core == core0)
        self.relay = (y != y0) & (core == core0)
        self.leaf = core != core0
        self.along = [
            remote(src, out, send.at[dy], recv.at[0], {"prow": (y + dy) % NY * 2 + core}) for dy in range(1, NY)
        ]
        self.own = remote(src, out, send.at[0], recv.at[0], {"prow": y * 2 + 1 - core})
        self.pass_on = remote(out, out, send.at[0], recv.at[0], {"prow": y * 2 + 1 - core})
        self.keep = pltpu.make_async_copy(src, out, send.at[NY])

    def start(self):
        @pl.when(self.owner)
        def _():
            for copy in self.along:
                copy.start()
            self.own.start()
            self.keep.start()

    def forward(self):
        @pl.when(self.relay)
        def _():
            self.pass_on.wait_recv()
            self.pass_on.start()

    def finish(self):
        @pl.when(self.relay)
        def _():
            self.pass_on.wait_send()

        @pl.when(self.leaf)
        def _():
            self.pass_on.wait_recv()

        @pl.when(self.owner)
        def _():
            for copy in self.along:
                copy.wait_send()
            self.own.wait_send()
            self.keep.wait()


def panel_kernel(slab_ref, a_ref, out_ref, top_ref, send, recv, tsend, trecv):
    _, _, x, z = place()
    rows = slab_ref.shape[0]
    out_ref[pl.ds(pl.multiple_of((x * NZ + z) * rows, rows), rows), :] = slab_ref[...]
    meet(gather_peers() + column_peers())
    top = Broadcast(0, 0, a_ref.at[pl.ds(0, top_ref.shape[0])], top_ref, tsend, trecv)
    top.start()
    gather(rows, out_ref, send, recv)
    top.forward()
    top.finish()


class Sum:
    def __init__(self, s, out, half, quarter, acc, send, recv):
        y, core, _, _ = place()
        self.s, self.out, self.half, self.quarter, self.acc, self.send, self.recv = s, out, half, quarter, acc, send, recv
        self.y, self.core = y, core
        self.width = s.shape[1]
        self.q = s.shape[0] // 8
        self.h = 4 * self.q
        self.mate = {"prow": y * 2 + 1 - core}
        self.own = self.rows(core * self.h + y * self.q, self.q)
        self.sent = []

    def rows(self, start, n):
        return pl.ds(pl.multiple_of(start, n), n)

    def copy(self, src, dst, i, peer):
        return remote(src, dst, self.send.at[i], self.recv.at[i], peer)

    def go(self, *args):
        copy = self.copy(*args)
        copy.start()
        self.sent.append(copy)
        return copy

    def along(self, dy):
        return {"prow": (self.y + dy) % NY * 2 + self.core}

    def exchange(self):
        self.first = self.go(self.s.at[self.rows((1 - self.core) * self.h, self.h)], self.half, 0, self.mate)

    def quarters(self):
        self.first.wait_recv()
        self.acc[...] = self.s[self.rows(self.core * self.h, self.h), :] + self.half[...]
        for dy in range(1, NY):
            piece = self.rows((self.y + dy) % NY * self.q, self.q)
            self.go(self.acc.at[piece], self.quarter.at[dy], dy, self.along(dy))

    def total(self):
        total = self.acc[self.rows(self.y * self.q, self.q), :]
        for dy in range(1, NY):
            self.copy(self.quarter.at[dy], self.quarter.at[dy], dy, self.mate).wait_recv()
            total = total + self.quarter[dy]
        self.out[self.own, pl.ds(0, self.width)] = total

    def spread(self):
        piece = self.out.at[self.own]
        for dy in range(1, NY):
            self.go(piece, piece, 3 + dy, self.along(dy))
        self.go(piece, piece, 7, self.mate)

    def forward(self):
        for dy in range(1, NY):
            piece = self.out.at[self.rows(self.core * self.h + (self.y + NY - dy) % NY * self.q, self.q)]
            self.copy(piece, piece, 3 + dy, self.mate).wait_recv()
            self.go(piece, piece, 7 + dy, self.mate)

    def finish(self):
        for dy in range(NY):
            piece = self.out.at[self.rows((1 - self.core) * self.h + (self.y + NY - dy) % NY * self.q, self.q)]
            self.copy(piece, piece, 7 + dy, self.mate).wait_recv()

    def flush(self):
        for copy in self.sent:
            copy.wait_send()


def main_kernel(
    pt_ref,
    ae_ref,
    a_ref,
    out_ref,
    c_ref,
    d_ref,
    b_ref,
    l_ref,
    a_buf,
    gram,
    gtop,
    ghalf,
    gquarter,
    gacc,
    aps,
    apt,
    ahalf,
    aquarter,
    aacc,
    av,
    avt,
    linv_s,
    t_s,
    vct_s,
    pct,
    mpart,
    mx,
    mz,
    mown,
    mraw,
    acopy,
    gsend,
    grecv,
    hsend,
    hrecv,
    asend,
    arecv,
    psend,
    precv,
    fsem,
    send,
    recv,
    xsend,
    xrecv,
    zsend,
    zrecv,
    xgsend,
    xgrecv,
    wsend,
    wrecv,
):
    y, core, x, z = place()
    prow, pcol = y * 2 + core, x * NZ + z
    nb = pt_ref.shape[0]
    cols = ae_ref.shape[1]
    h, q = nb // 2, nb // 8
    rows = cols // 8

    load = pltpu.make_async_copy(a_ref, a_buf, acopy.at[0])
    load.start()

    to_row, to_col = pcol // 4, pcol % 4 * 8 + prow
    from_col, from_row = prow * 4 + pcol // 8, pcol % 8
    stays = (to_row == prow) & (to_col == pcol)
    moves = jnp.logical_not(stays)
    target = {"prow": to_row, "pcol": to_col}
    source = {"prow": from_row, "pcol": from_col}
    barrier = pltpu.get_barrier_semaphore()
    peers = [{"prow": (prow + d) % 8} for d in range(1, 8)]
    peers += [{"pcol": (x + dx) % NX * NZ + z} for dx in range(1, NX)]
    peers += [{"pcol": x * NZ + (z + dz) % NZ} for dz in range(1, NZ)]

    def greet(peer):
        pl.semaphore_signal(barrier, inc=1, device_id=peer, device_id_type=pl.DeviceIdType.MESH)

    for peer in peers:
        greet(peer)

    @pl.when(moves)
    def _():
        greet(target)
        greet(source)

    gram[...] = mm(pt_ref[...], pt_ref[...], NT)

    @pl.when(moves)
    def _():
        pl.semaphore_wait(barrier, len(peers) + 2)

    @pl.when(stays)
    def _():
        pl.semaphore_wait(barrier, len(peers))

    gsum = Sum(gram, gtop, ghalf, gquarter, gacc, gsend, grecv)
    asum = Sum(aps, apt, ahalf, aquarter, aacc, asend, arecv)
    gsum.exchange()
    handed = []
    for r in range(1, 8):
        piece = pl.ds(r % 2 * h + r // 2 * q, q)
        src, dst = pt_ref.at[piece, pl.ds(0, nb)], gtop.at[piece, pl.ds(nb, nb)]
        handed.append(remote(src, dst, hsend.at[r], hrecv.at[0], {"prow": r}))

    @pl.when(prow == 0)
    def _():
        for copy in handed:
            copy.start()
        gtop[pl.ds(0, q), pl.ds(nb, nb)] = pt_ref[pl.ds(0, q), pl.ds(0, nb)]

    load.wait()

    def product(half):
        mine = gsum.rows(half * h, h)
        aps[mine, :] = mm3(split(pt_ref[mine, :]), split(a_buf[...]))

    product(1 - core)
    asum.exchange()
    gsum.quarters()
    product(core)
    gsum.total()

    @pl.when(prow != 0)
    def _():
        piece = gtop.at[gsum.own, pl.ds(nb, nb)]
        remote(piece, piece, hsend.at[0], hrecv.at[0], gsum.mate).wait_recv()

    gsum.spread()
    asum.quarters()
    gsum.forward()
    gsum.finish()

    offset = pl.multiple_of(pcol % 4 * cols, cols)
    part = Broadcast(x, z // 4, pt_ref.at[:, pl.ds(offset, cols)], pct, psend, precv)

    def first():
        asum.total()
        asum.spread()
        part.start()

    stages = iter([first, asum.forward, lambda: None, lambda: None])
    linv = lower_inverse(gtop[:, 0:nb], lambda: next(stages)())
    linv_s[...] = linv
    asum.finish()
    avt[...] = mm(linv, apt[...]) - ae_ref[...]
    av[...] = avt[...].T

    mine = pl.ds(pl.multiple_of(prow * rows, rows), rows)
    swap = remote(
        av.at[mine], out_ref.at[pl.ds(pl.multiple_of(to_col * rows, rows), rows)], fsem.at[0], fsem.at[1], target
    )

    @pl.when(moves)
    def _():
        swap.start()

    @pl.when(stays)
    def _():
        out_ref[pl.ds(pl.multiple_of(pcol * rows, rows), rows), :] = av[mine, :]

    part.forward()
    part.finish()

    @pl.when(moves)
    def _():
        swap.wait_recv()

    def along_x(src, dst, sends, recvs, dx):
        return remote(src, dst, sends.at[dx], recvs.at[dx], {"pcol": (x + dx) % NX * NZ + z})

    def m_first():
        e = (iota((nb, cols), 0) == iota((nb, cols), 1)) & (pcol == 0)
        vct_s[...] = mm(linv_s[...], pct[...]) - e.astype(F32)
        mpart[...] = mm(vct_s[pl.ds(pl.multiple_of(prow * q, q), q), :], av[...])
        for dx in range(1, NX):
            piece = pl.ds(pl.multiple_of((x + dx) % NX * 8, 8), 8)
            along_x(mpart.at[piece], mx.at[dx], xsend, xrecv, dx).start()

    def factor():
        linv = linv_s[...]
        side = mm(linv, gtop[:, nb:])
        r, c = iota((nb, nb), 0), iota((nb, nb), 1)
        ygram = 2.0 * (r == c).astype(F32) - side - mm(gtop[:, nb:], linv, ((0,), (1,)))
        t_s[...] = upper_inverse(jnp.where(r < c, ygram, jnp.where(r == c, 0.5 * ygram, 0.0)))

    def m_second():
        total = mpart[pl.ds(pl.multiple_of(x * 8, 8), 8), :]
        for dx in range(1, NX):
            along_x(mx.at[dx], mx.at[dx], xsend, xrecv, dx).wait_recv()
            total = total + mx[dx]
        mown[...] = total
        for dz in range(1, NZ):
            remote(mown, mz.at[dz], zsend.at[dz], zrecv.at[dz], {"pcol": x * NZ + (z + dz) % NZ}).start()

    m_own = mraw.at[pl.ds(pl.multiple_of(prow * q + x * 8, 8), 8)]
    m_rows = mraw.at[pl.ds(pl.multiple_of(prow * q, q), q)]

    def m_third():
        total = mown[...]
        for dz in range(1, NZ):
            remote(mown, mz.at[dz], zsend.at[dz], zrecv.at[dz], {"pcol": x * NZ + (z + dz) % NZ}).wait_recv()
            total = total + mz[dz]
        mraw[pl.ds(pl.multiple_of(prow * q + x * 8, 8), 8), :] = total
        for dx in range(1, NX):
            along_x(m_own, m_own, xgsend, xgrecv, dx).start()

    def m_fourth():
        for dx in range(1, NX):
            along_x(m_own, m_own, xgsend, xgrecv, dx).wait_recv()
        for d in range(1, 8):
            remote(m_rows, m_rows, wsend.at[d], wrecv.at[d], {"prow": (prow + d) % 8}).start()

    def last():
        for d in range(1, 8):
            remote(m_rows, m_rows, wsend.at[d], wrecv.at[d], {"prow": (prow + d) % 8}).wait_recv()
        t, vct, linv = t_s[...], vct_s[...], linv_s[...]
        k = mm(t, mm(mraw[...], t), TN)
        b = mm(t, avt[...], TN) - mm(0.5 * (k + k.T), vct)
        b_ref[...] = b
        c_ref[...] = mm(linv, b, TN)
        d_ref[...] = mm(t, vct)
        sel = (iota((8, nb), 1) == iota((8, nb), 0) + 8 * pcol).astype(F32)
        kt = mm(sel, k, NT)
        l_ref[0:8, :] = kt
        l_ref[8:16, :] = mm(kt, linv)
        l_ref[16:24, :] = mm(sel, t, NT)

    gather(rows, out_ref, send, recv, (m_first, factor, m_second, m_third, m_fourth, last))

    gsum.flush()
    asum.flush()

    @pl.when(prow == 0)
    def _():
        for copy in handed:
            copy.wait_send()

    @pl.when(moves)
    def _():
        swap.wait_send()

    for dx in range(1, NX):
        along_x(mpart.at[pl.ds(0, 8)], mx.at[dx], xsend, xrecv, dx).wait_send()
        along_x(m_own, m_own, xgsend, xgrecv, dx).wait_send()
    for dz in range(1, NZ):
        remote(mown, mz.at[dz], zsend.at[dz], zrecv.at[dz], {"pcol": x * NZ + (z + dz) % NZ}).wait_send()
    for d in range(1, 8):
        remote(m_rows, m_rows, wsend.at[d], wrecv.at[d], {"prow": (prow + d) % 8}).wait_send()


def params(cid):
    return pltpu.CompilerParams(collective_id=cid, has_side_effects=True, vmem_limit_bytes=LIMIT)


def plain(**kw):
    return pltpu.CompilerParams(vmem_limit_bytes=LIMIT, **kw)


def shape(*dims):
    return jax.ShapeDtypeStruct(dims, F32)


def update_kernel(a_ref, pt_ref, av_ref, c_ref, d_ref, b_ref, l_ref, o_ref, w_ref, ch, cl, dh, dl):
    step = pl.program_id(0)

    @pl.when(step == 0)
    def _():
        ch[...], cl[...] = split(c_ref[...])
        dh[...], dl[...] = split(d_ref[...])

    p, v = pt_ref[...], av_ref[...]
    both = mm3(split(p), (ch[...], cl[...]), TN) + mm3(split(v), (dh[...], dl[...]))
    o_ref[...] = a_ref[...] - both
    w_ref[...] = mm(l_ref[16:24, :], v, NT) - 0.5 * mm(l_ref[8:16, :], p)

    @pl.when((lax.axis_index("prow") == 0) & (step == 0))
    def _():
        o_ref[...] += b_ref[...]
        w_ref[...] += 0.5 * l_ref[0:8, :]


def shards(trailing, panel):
    rows, cols = trailing.shape
    pt_own = panel.T
    nc = pt_own.shape[0]
    nb = nc * lax.axis_size("pcol")
    dma = pltpu.SemaphoreType.DMA
    buf = lambda *dims: pltpu.VMEM(dims, F32)

    pt, ae = pl.pallas_call(
        panel_kernel,
        out_shape=(shape(nb, rows), shape(nb, cols)),
        in_specs=[VMEM, ANY],
        out_specs=(VMEM, VMEM),
        scratch_shapes=[dma((NX, NZ)), dma((NX, NZ)), dma((NY + 1,)), dma((1,))],
        compiler_params=params(1),
    )(pt_own, trailing)

    h, q = nb // 2, nb // 8
    av, c, d, b, l = pl.pallas_call(
        main_kernel,
        out_shape=(shape(rows, nb),) + (shape(nb, cols),) * 3 + (shape(24, nb),),
        in_specs=[VMEM, VMEM, ANY],
        out_specs=(VMEM,) * 5,
        scratch_shapes=[
            buf(rows, cols),
            buf(nb, nb),
            buf(nb, 2 * nb),
            buf(h, nb),
            buf(NY, q, nb),
            buf(h, nb),
            buf(nb, cols),
            buf(nb, cols),
            buf(h, cols),
            buf(NY, q, cols),
            buf(h, cols),
            buf(cols, nb),
            buf(nb, cols),
            buf(nb, nb),
            buf(nb, nb),
            buf(nb, cols),
            buf(nb, cols),
            buf(q, nb),
            buf(NX, 8, nb),
            buf(NZ, 8, nb),
            buf(8, nb),
            buf(nb, nb),
            dma((1,)),
            dma((11,)),
            dma((11,)),
            dma((8,)),
            dma((1,)),
            dma((11,)),
            dma((11,)),
            dma((NY + 1,)),
            dma((1,)),
            dma((2,)),
            dma((NX, NZ)),
            dma((NX, NZ)),
            dma((NX,)),
            dma((NX,)),
            dma((NZ,)),
            dma((NZ,)),
            dma((NX,)),
            dma((NX,)),
            dma((8,)),
            dma((8,)),
        ],
        compiler_params=params(2),
    )(pt, ae, trailing)

    tile = nb
    whole = lambda *dims: pl.BlockSpec(dims, lambda i: (0, 0))
    updated, wt = pl.pallas_call(
        update_kernel,
        grid=(rows // tile,),
        out_shape=(shape(rows, cols), shape(nc, rows)),
        in_specs=[
            pl.BlockSpec((tile, cols), lambda i: (i, 0)),
            pl.BlockSpec((nb, tile), lambda i: (0, i)),
            pl.BlockSpec((tile, nb), lambda i: (i, 0)),
            whole(nb, cols),
            whole(nb, cols),
            whole(nb, cols),
            whole(24, nb),
        ],
        out_specs=(pl.BlockSpec((tile, cols), lambda i: (i, 0)), pl.BlockSpec((nc, tile), lambda i: (0, i))),
        scratch_shapes=[pltpu.VMEM((nb, cols), jnp.bfloat16)] * 4,
        compiler_params=plain(dimension_semantics=("arbitrary",)),
    )(trailing, pt, av, c, d, b, l)
    return updated, wt.T


def solution(mesh):
    in_specs = (P("prow", "pcol"), P("prow", "pcol"))
    out_specs = (P("prow", "pcol"), P("prow", "pcol"))
    return jax.shard_map(shards, mesh=mesh, in_specs=in_specs, out_specs=out_specs, check_vma=False)
```

time: 141 us -> 127 us (0.901)
  the two profiles are of different devices: /device:TPU:1 before, /device:TPU:6 now
where the time goes in v1:
time: 127 us
  Pallas kernels  124 us (98%)
  local copies, waits for them, and re-layouts  2.15 us (2%)
    pallas_call x1, Pallas kernels, shards(): pl.pallas_call(main_kernel, out_shape=(shape(rows, nb),) + (shape(nb, col...  85.8 us
    pallas_call x1, Pallas kernels, shards(): pl.pallas_call(panel_kernel, out_shape=(shape(nb, rows), shape(nb, cols))...  28 us
    pallas_call x1, Pallas kernels, shards(): pl.pallas_call(update_kernel, grid=(rows // tile,), out_shape=(shape(rows...  10.3 us

profile of v1, /device:TPU:6, one launch (start us, length us, event | category | flops | bytes accessed | tf_op | source)
XLA Modules:
  0.0 126.9 jit_solution(12133218267208539061)
XLA Ops:
  0.6 0.0 copy-start.2
  0.6 0.8 copy-done.2
  1.5 28.0 %shard_map.41 = (f32[256,2048]{1,0:T(8,128)S(1)}, f32[256,512]{1,0:T(8,128)S(1)}) custom-call(f32[8,2048]{1,0:T(8,128)S(1)} %bitcast.2, f32[2048,512]{1,0:T(8,128)} %a_ref.5), custom_call_target="tpu_custom_call" | custom-call | tf_op jit(solution)/shard_map/pallas_call | solution.py:662
  29.5 0.0 copy-start
  29.5 1.3 %copy-done = f32[256,2048]{1,0:T(8,128)} copy-done((f32[256,2048]{1,0:T(8,128)}, f32[256,2048]{1,0:T(8,128)S(1)}, u32[]{:S(2)}) %copy-start) | copy-done | bytes 2097176
  30.8 0.0 copy-start.1
  30.9 85.8 %shard_map.42 = (f32[2048,256]{1,0:T(8,128)S(1)}, f32[256,512]{1,0:T(8,128)S(1)}, f32[256,512]{1,0:T(8,128)S(1)}, f32[256,512]{1,0:T(8,128)S(1)}, f32[24,256]{1,0:T(8,128)S(1)}) custom-call(f32[256,2048]{1,0:T(8,128)} %copy-done, f32[256,512]{1,0:T(8,128)S(1)} %get-tuple-element.12.ae_ref, f32[2048,512]{1,0:T(8,128)} %a_ref.5), custom_call_target="tpu_custom_call" | custom-call | tf_op jit(solution)/shard_map/pallas_call | solution.py:672
  116.6 0.0 copy-done.1
  116.6 10.3 %shard_map.43 = (f32[2048,512]{1,0:T(8,128)}, f32[8,2048]{1,0:T(8,128)}) custom-call(f32[2048,512]{1,0:T(8,128)} %a_ref.5, f32[256,2048]{1,0:T(8,128)S(1)} %copy-done.1, f32[2048,256]{1,0:T(8,128)S(1)} %get-tuple-element.13.av_ref, f32[256,512]{1,0:T(8,128)S(1)} %get-tuple-element.14.c_ref, f32[256,512]{1,0:T(8,128)S(1)} %get-tuple-element.15.d_ref, ...), custom_call_target="tpu_custom_call" | custom-call | tf_op jit(solution)/shard_map/pallas_call | solution.py:726
Async XLA Ops:
  0.6 0.8 copy-start.2
  29.5 1.3 %copy-start = (f32[256,2048]{1,0:T(8,128)}, f32[256,2048]{1,0:T(8,128)S(1)}, u32[]{:S(2)}) copy-start(f32[256,2048]{1,0:T(8,128)S(1)} %get-tuple-element.11.pt_ref) | copy-start | bytes 6291460
  30.8 85.8 %copy-start.1 = (f32[256,2048]{1,0:T(8,128)S(1)}, f32[256,2048]{1,0:T(8,128)}, u32[]{:S(2)}) copy-start(f32[256,2048]{1,0:T(8,128)} %copy-done) | copy-start | bytes 6291460

commit v2 on v1

--- a/solution.py
+++ b/solution.py
@@ -130,25 +130,6 @@
     return inv
 
 
-def upper_inverse(y):
-    size = y.shape[0]
-    if size == BASE:
-        return upper_base(y)
-    h = size // 2
-    i_top = upper_inverse(y[:h, :h])
-    i_bot = upper_inverse(y[h:, h:])
-    i_side = -mm(i_top, mm(y[:h, h:], i_bot))
-    bottom = jnp.concatenate([jnp.zeros((h, h), F32), i_bot], 1)
-    return jnp.concatenate([jnp.concatenate([i_top, i_side], 1), bottom], 0)
-
-
-def meet(peers):
-    barrier = pltpu.get_barrier_semaphore()
-    for peer in peers:
-        pl.semaphore_signal(barrier, inc=1, device_id=peer, device_id_type=pl.DeviceIdType.MESH)
-    pl.semaphore_wait(barrier, len(peers))
-
-
 def remote(src, dst, send, recv, peer):
     return pltpu.make_async_remote_copy(
         src_ref=src, dst_ref=dst, send_sem=send, recv_sem=recv, device_id=peer, device_id_type=pl.DeviceIdType.MESH
@@ -160,18 +141,14 @@
     return prow // 2, prow % 2, pcol // NZ, pcol % NZ
 
 
-def gather_peers():
-    _, _, x, z = place()
-    peers = [{"pcol": x * NZ + (z + 1) % NZ}, {"pcol": x * NZ + (z + NZ - 1) % NZ}]
-    return peers + [{"pcol": (x + dx) % NX * NZ + z} for dx in range(1, NX)]
-
-
-def gather(rows, out, send, recv, hooks=()):
+ORDER = (1, 7, 2, 6, 3, 5, 4)
+
+
+def gather(at, send, recv, hooks=()):
     _, core, x, z = place()
 
     def slab(xx, zz):
-        start = (xx % NX * NZ + (zz + 2 * NZ) % NZ) * rows
-        return out.at[pl.ds(pl.multiple_of(start, rows), rows)]
+        return at(xx % NX, (zz + 2 * NZ) % NZ)
 
     def along_z(dx, dist):
         step = 1 if dist <= NZ // 2 else -1
@@ -191,8 +168,6 @@
             along_z(dx, dist + 1).start()
         elif dist > NZ // 2 + 1:
             along_z(dx, dist - 1).start()
-
-    order = (1, 7, 2, 6, 3, 5, 4)
 
     @pl.when(core == 0)
     def _():
@@ -212,7 +187,7 @@
             along_z(dx, 1).start()
             along_z(dx, NZ - 1).start()
 
-    for i, dist in enumerate(order):
+    for i, dist in enumerate(ORDER):
 
         @pl.when(core == 0)
         def _():
@@ -220,6 +195,8 @@
             passed_on(0, dist)
             for dx in range(1, NX):
                 along_x(dx, dist).start()
+            for dx in range(1, NX):
+                arrived(dx, ORDER[i - 1] if i else 0)
 
         @pl.when(core == 1)
         def _():
@@ -232,21 +209,17 @@
 
     @pl.when(core == 0)
     def _():
-        for dist in (0,) + order:
-            for dx in range(1, NX):
-                arrived(dx, dist)
-
-    for dx in range(NX):
-        for dist in range(NZ):
-            if dx or dist:
-                piece = slab(x, z)
-                remote(piece, piece, send.at[dx, dist], recv.at[dx, dist], {"pcol": x * NZ + (z + 1) % NZ}).wait_send()
-
-
-def column_peers():
-    y, core, _, _ = place()
-    peers = [{"prow": (y + dy) % NY * 2 + core} for dy in range(1, NY)]
-    return peers + [{"prow": y * 2 + 1 - core}]
+        for dx in range(1, NX):
+            arrived(dx, ORDER[-1])
+
+    def flush():
+        for dx in range(NX):
+            for dist in range(NZ):
+                if dx or dist:
+                    piece = slab(x, z)
+                    remote(piece, piece, send.at[dx, dist], recv.at[dx, dist], {"pcol": x * NZ + (z + 1) % NZ}).wait_send()
+
+    return flush
 
 
 class Broadcast:
@@ -293,16 +266,57 @@
             self.keep.wait()
 
 
-def panel_kernel(slab_ref, a_ref, out_ref, top_ref, send, recv, tsend, trecv):
-    _, _, x, z = place()
-    rows = slab_ref.shape[0]
-    out_ref[pl.ds(pl.multiple_of((x * NZ + z) * rows, rows), rows), :] = slab_ref[...]
-    meet(gather_peers() + column_peers())
-    top = Broadcast(0, 0, a_ref.at[pl.ds(0, top_ref.shape[0])], top_ref, tsend, trecv)
-    top.start()
-    gather(rows, out_ref, send, recv)
-    top.forward()
-    top.finish()
+class Parts:
+    def __init__(self, y0, core0, src, window, out, send, recv):
+        y, core, _, z = place()
+        self.owner = (y == y0) & (core == core0)
+        self.relay = (y != y0) & (core == core0)
+        self.leaf = core != core0
+        self.src, self.window, self.out, self.send, self.recv, self.y, self.core, self.z = src, window, out, send, recv, y, core, z
+
+    def rows(self, dist):
+        return pl.ds(pl.multiple_of((self.z + NZ - dist) % NZ * 8, 8), 8)
+
+    def copy(self, dist, dy, passed=False):
+        rows = self.rows(dist)
+        dst = self.out.at[:, rows]
+        src = dst if passed else self.src.at[:, rows, self.window]
+        peer = (self.y + dy) % NY * 2 + self.core if dy else self.y * 2 + 1 - self.core
+        return remote(src, dst, self.send.at[dist, dy], self.recv.at[dist], {"prow": peer})
+
+    def start(self, dist):
+        @pl.when(self.owner)
+        def _():
+            for dy in (1, 3, 2, 0):
+                self.copy(dist, dy).start()
+
+    def forward(self, dist):
+        @pl.when(self.relay)
+        def _():
+            self.copy(dist, 0, True).wait_recv()
+            self.copy(dist, 0, True).start()
+
+    def finish(self):
+        @pl.when(self.owner)
+        def _():
+            self.out[...] = self.src[:, :, self.window]
+
+        @pl.when(self.leaf)
+        def _():
+            for dist in range(NZ):
+                self.copy(dist, 0, True).wait_recv()
+
+    def flush(self):
+        @pl.when(self.owner)
+        def _():
+            for dist in range(NZ):
+                for dy in range(NY):
+                    self.copy(dist, dy).wait_send()
+
+        @pl.when(self.relay)
+        def _():
+            for dist in range(NZ):
+                self.copy(dist, 0, True).wait_send()
 
 
 class Sum:
@@ -372,15 +386,18 @@
 
 
 def main_kernel(
+    slab_ref,
+    a_ref,
     pt_ref,
-    ae_ref,
-    a_ref,
     out_ref,
     c_ref,
     d_ref,
     b_ref,
     l_ref,
     a_buf,
+    a_hi,
+    a_lo,
+    ae,
     gram,
     gtop,
     ghalf,
@@ -403,6 +420,10 @@
     mown,
     mraw,
     acopy,
+    panel_send,
+    panel_recv,
+    esend,
+    erecv,
     gsend,
     grecv,
     hsend,
@@ -425,10 +446,11 @@
 ):
     y, core, x, z = place()
     prow, pcol = y * 2 + core, x * NZ + z
-    nb = pt_ref.shape[0]
-    cols = ae_ref.shape[1]
+    nb = out_ref.shape[1]
+    cols = ae.shape[1]
     h, q = nb // 2, nb // 8
     rows = cols // 8
+    wide = slab_ref.shape[1]
 
     load = pltpu.make_async_copy(a_ref, a_buf, acopy.at[0])
     load.start()
@@ -455,7 +477,7 @@
         greet(target)
         greet(source)
 
-    gram[...] = mm(pt_ref[...], pt_ref[...], NT)
+    pt_ref[x, pl.ds(pl.multiple_of(z * 8, 8), 8), :] = slab_ref[...]
 
     @pl.when(moves)
     def _():
@@ -464,6 +486,38 @@
     @pl.when(stays)
     def _():
         pl.semaphore_wait(barrier, len(peers))
+
+    top = Broadcast(0, 0, a_ref.at[pl.ds(0, nb)], ae, esend, erecv)
+    top.start()
+    window = pl.ds(pl.multiple_of(pcol % 4 * cols, cols), cols)
+    part = Parts(x, z // 4, pt_ref, window, pct, psend, precv)
+
+    def split_a():
+        load.wait()
+        a_hi[...], a_lo[...] = split(a_buf[...])
+
+    def step(i):
+        def run():
+            part.start(((0,) + ORDER)[i])
+            if i:
+                part.forward(((0,) + ORDER)[i - 1])
+            if i == 1:
+                split_a()
+            if i == 4:
+                top.forward()
+
+        return run
+
+    panel_flush = gather(
+        lambda xx, zz: pt_ref.at[xx, pl.ds(pl.multiple_of(zz * 8, 8), 8)],
+        panel_send,
+        panel_recv,
+        [step(i) for i in range(7)],
+    )
+    part.start(ORDER[6])
+    part.forward(ORDER[5])
+    panel = pt_ref[...].reshape(nb, wide)
+    gram[...] = mm(panel, panel, NT)
 
     gsum = Sum(gram, gtop, ghalf, gquarter, gacc, gsend, grecv)
     asum = Sum(aps, apt, ahalf, aquarter, aacc, asend, arecv)
@@ -471,20 +525,19 @@
     handed = []
     for r in range(1, 8):
         piece = pl.ds(r % 2 * h + r // 2 * q, q)
-        src, dst = pt_ref.at[piece, pl.ds(0, nb)], gtop.at[piece, pl.ds(nb, nb)]
+        src = pt_ref.at[(r % 2 * h + r // 2 * q) // 64, pl.ds((r % 2 * h + r // 2 * q) % 64, q), pl.ds(0, nb)]
+        dst = gtop.at[piece, pl.ds(nb, nb)]
         handed.append(remote(src, dst, hsend.at[r], hrecv.at[0], {"prow": r}))
 
     @pl.when(prow == 0)
     def _():
         for copy in handed:
             copy.start()
-        gtop[pl.ds(0, q), pl.ds(nb, nb)] = pt_ref[pl.ds(0, q), pl.ds(0, nb)]
-
-    load.wait()
+        gtop[pl.ds(0, q), pl.ds(nb, nb)] = pt_ref[0, pl.ds(0, q), pl.ds(0, nb)]
 
     def product(half):
-        mine = gsum.rows(half * h, h)
-        aps[mine, :] = mm3(split(pt_ref[mine, :]), split(a_buf[...]))
+        mine = pt_ref[pl.ds(half * 2, 2)].reshape(h, wide)
+        aps[gsum.rows(half * h, h), :] = mm3(split(mine), (a_hi[...], a_lo[...]))
 
     product(1 - core)
     asum.exchange()
@@ -502,19 +555,22 @@
     gsum.forward()
     gsum.finish()
 
-    offset = pl.multiple_of(pcol % 4 * cols, cols)
-    part = Broadcast(x, z // 4, pt_ref.at[:, pl.ds(offset, cols)], pct, psend, precv)
-
     def first():
         asum.total()
         asum.spread()
-        part.start()
-
-    stages = iter([first, asum.forward, lambda: None, lambda: None])
+
+    def second():
+        asum.forward()
+        part.forward(ORDER[6])
+
+    def third():
+        asum.finish()
+        part.finish()
+
+    stages = iter([first, second, third, top.finish])
     linv = lower_inverse(gtop[:, 0:nb], lambda: next(stages)())
     linv_s[...] = linv
-    asum.finish()
-    avt[...] = mm(linv, apt[...]) - ae_ref[...]
+    avt[...] = mm(linv, apt[...]) - ae[...]
     av[...] = avt[...].T
 
     mine = pl.ds(pl.multiple_of(prow * rows, rows), rows)
@@ -530,9 +586,6 @@
     def _():
         out_ref[pl.ds(pl.multiple_of(pcol * rows, rows), rows), :] = av[mine, :]
 
-    part.forward()
-    part.finish()
-
     @pl.when(moves)
     def _():
         swap.wait_recv()
@@ -542,18 +595,32 @@
 
     def m_first():
         e = (iota((nb, cols), 0) == iota((nb, cols), 1)) & (pcol == 0)
-        vct_s[...] = mm(linv_s[...], pct[...]) - e.astype(F32)
+        vct_s[...] = mm(linv_s[...], pct[...].reshape(nb, cols)) - e.astype(F32)
         mpart[...] = mm(vct_s[pl.ds(pl.multiple_of(prow * q, q), q), :], av[...])
         for dx in range(1, NX):
             piece = pl.ds(pl.multiple_of((x + dx) % NX * 8, 8), 8)
             along_x(mpart.at[piece], mx.at[dx], xsend, xrecv, dx).start()
 
-    def factor():
+    def factor_first():
         linv = linv_s[...]
         side = mm(linv, gtop[:, nb:])
         r, c = iota((nb, nb), 0), iota((nb, nb), 1)
         ygram = 2.0 * (r == c).astype(F32) - side - mm(gtop[:, nb:], linv, ((0,), (1,)))
-        t_s[...] = upper_inverse(jnp.where(r < c, ygram, jnp.where(r == c, 0.5 * ygram, 0.0)))
+        t_s[...] = jnp.where(r < c, ygram, jnp.where(r == c, 0.5 * ygram, 0.0))
+
+    def factor_second():
+        blocks = [slice(k * BASE, (k + 1) * BASE) for k in range(nb // BASE)]
+        inverses = [upper_base(t_s[k, k]) for k in blocks]
+        for k, inverse in zip(blocks, inverses):
+            t_s[k, k] = inverse
+
+    def merge(size):
+        sides = []
+        for k in range(0, nb, 2 * size):
+            lo, hi = slice(k, k + size), slice(k + size, k + 2 * size)
+            sides.append((lo, hi, -mm(t_s[lo, lo], mm(t_s[lo, hi], t_s[hi, hi]))))
+        for lo, hi, side in sides:
+            t_s[lo, hi] = side
 
     def m_second():
         total = mpart[pl.ds(pl.multiple_of(x * 8, 8), 8), :]
@@ -597,7 +664,23 @@
         l_ref[8:16, :] = mm(kt, linv)
         l_ref[16:24, :] = mm(sel, t, NT)
 
-    gather(rows, out_ref, send, recv, (m_first, factor, m_second, m_third, m_fourth, last))
+    def fourth():
+        merge(BASE)
+        m_second()
+
+    def fifth():
+        merge(2 * BASE)
+        m_third()
+
+    flush = gather(
+        lambda xx, zz: out_ref.at[pl.ds(pl.multiple_of((xx * NZ + zz) * rows, rows), rows)],
+        send,
+        recv,
+        (m_first, factor_first, factor_second, fourth, fifth, m_fourth, last),
+    )
+    flush()
+    panel_flush()
+    part.flush()
 
     gsum.flush()
     asum.flush()
@@ -641,14 +724,16 @@
         dh[...], dl[...] = split(d_ref[...])
 
     p, v = pt_ref[...], av_ref[...]
-    both = mm3(split(p), (ch[...], cl[...]), TN) + mm3(split(v), (dh[...], dl[...]))
+    ps, vs = split(p), split(v)
+    both = mm3(ps, (ch[...], cl[...]), TN) + mm3(vs, (dh[...], dl[...]))
     o_ref[...] = a_ref[...] - both
-    w_ref[...] = mm(l_ref[16:24, :], v, NT) - 0.5 * mm(l_ref[8:16, :], p)
+    w_ref[...] = mm3(split(l_ref[16:24, :]), vs, NT) - 0.5 * mm3(split(l_ref[8:16, :]), ps)
 
     @pl.when((lax.axis_index("prow") == 0) & (step == 0))
     def _():
-        o_ref[...] += b_ref[...]
-        w_ref[...] += 0.5 * l_ref[0:8, :]
+        nb = b_ref.shape[0]
+        o_ref[0:nb, :] += b_ref[...]
+        w_ref[:, 0:nb] += 0.5 * l_ref[0:8, :]
 
 
 def shards(trailing, panel):
@@ -659,23 +744,17 @@
     dma = pltpu.SemaphoreType.DMA
     buf = lambda *dims: pltpu.VMEM(dims, F32)
 
-    pt, ae = pl.pallas_call(
-        panel_kernel,
-        out_shape=(shape(nb, rows), shape(nb, cols)),
+    h, q = nb // 2, nb // 8
+    pt, av, c, d, b, l = pl.pallas_call(
+        main_kernel,
+        out_shape=(shape(NX, nb // NX, rows), shape(rows, nb)) + (shape(nb, cols),) * 3 + (shape(24, nb),),
         in_specs=[VMEM, ANY],
-        out_specs=(VMEM, VMEM),
-        scratch_shapes=[dma((NX, NZ)), dma((NX, NZ)), dma((NY + 1,)), dma((1,))],
-        compiler_params=params(1),
-    )(pt_own, trailing)
-
-    h, q = nb // 2, nb // 8
-    av, c, d, b, l = pl.pallas_call(
-        main_kernel,
-        out_shape=(shape(rows, nb),) + (shape(nb, cols),) * 3 + (shape(24, nb),),
-        in_specs=[VMEM, VMEM, ANY],
-        out_specs=(VMEM,) * 5,
+        out_specs=(VMEM,) * 6,
         scratch_shapes=[
             buf(rows, cols),
+            pltpu.VMEM((rows, cols), jnp.bfloat16),
+            pltpu.VMEM((rows, cols), jnp.bfloat16),
+            buf(nb, cols),
             buf(nb, nb),
             buf(nb, 2 * nb),
             buf(h, nb),
@@ -691,12 +770,16 @@
             buf(nb, nb),
             buf(nb, nb),
             buf(nb, cols),
-            buf(nb, cols),
+            buf(NX, nb // NX, cols),
             buf(q, nb),
             buf(NX, 8, nb),
             buf(NZ, 8, nb),
             buf(8, nb),
             buf(nb, nb),
+            dma((1,)),
+            dma((NX, NZ)),
+            dma((NX, NZ)),
+            dma((NY + 1,)),
             dma((1,)),
             dma((11,)),
             dma((11,)),
@@ -704,8 +787,8 @@
             dma((1,)),
             dma((11,)),
             dma((11,)),
-            dma((NY + 1,)),
-            dma((1,)),
+            dma((NZ, NY)),
+            dma((NZ,)),
             dma((2,)),
             dma((NX, NZ)),
             dma((NX, NZ)),
@@ -719,9 +802,9 @@
             dma((8,)),
         ],
         compiler_params=params(2),
-    )(pt, ae, trailing)
-
-    tile = nb
+    )(pt_own, trailing)
+
+    tile = 2 * nb
     whole = lambda *dims: pl.BlockSpec(dims, lambda i: (0, 0))
     updated, wt = pl.pallas_call(
         update_kernel,
@@ -739,7 +822,7 @@
         out_specs=(pl.BlockSpec((tile, cols), lambda i: (i, 0)), pl.BlockSpec((nc, tile), lambda i: (0, i))),
         scratch_shapes=[pltpu.VMEM((nb, cols), jnp.bfloat16)] * 4,
         compiler_params=plain(dimension_semantics=("arbitrary",)),
-    )(trailing, pt, av, c, d, b, l)
+    )(trailing, pt.reshape(nb, rows), av, c, d, b, l)
     return updated, wt.T
 
 

time: 127 us -> 130 us (1.024)
  the two profiles are of different devices: /device:TPU:6 before, /device:TPU:1 now
where the time goes in v2:
time: 130 us
  Pallas kernels  128 us (98%)
    pallas_call x1, Pallas kernels, shards(): pl.pallas_call(main_kernel, out_shape=(shape(NX, nb // NX, rows), shape(r...  121 us
    pallas_call x1, Pallas kernels, shards(): pl.pallas_call(update_kernel, grid=(rows // tile,), out_shape=(shape(rows...  7.9 us

profile of v2, /device:TPU:1, one launch (start us, length us, event | category | flops | bytes accessed | tf_op | source)
XLA Modules:
  0.0 129.9 jit_solution(11347702204369536076)
XLA Ops:
  0.6 0.0 copy-start
  0.6 0.8 copy-done
  1.5 120.6 %shard_map.41 = (f32[4,64,2048]{2,1,0:T(8,128)S(1)}, f32[2048,256]{1,0:T(8,128)S(1)}, f32[256,512]{1,0:T(8,128)S(1)}, f32[256,512]{1,0:T(8,128)S(1)}, f32[256,512]{1,0:T(8,128)S(1)}, /*index=5*/f32[24,256]{1,0:T(8,128)S(1)}) custom-call(f32[8,2048]{1,0:T(8,128)S(1)} %bitcast.4, f32[2048,512]{1,0:T(8,128)} %a_ref.3), custom_call_target="tpu_custom_call" | custom-call | tf_op jit(solution)/shard_map/pallas_call | solution.py:748
  122.0 7.9 %shard_map.42 = (f32[2048,512]{1,0:T(8,128)}, f32[8,2048]{1,0:T(8,128)}) custom-call(f32[2048,512]{1,0:T(8,128)} %a_ref.3, f32[256,2048]{1,0:T(8,128)S(1)} %bitcast.3, f32[2048,256]{1,0:T(8,128)S(1)} %get-tuple-element.11.av_ref, f32[256,512]{1,0:T(8,128)S(1)} %get-tuple-element.12.c_ref, f32[256,512]{1,0:T(8,128)S(1)} %get-tuple-element.13.d_ref, ...), custom_call_target="tpu_custom_call" | custom-call | tf_op jit(solution)/shard_map/pallas_call | solution.py:809
Async XLA Ops:
  0.6 0.8 copy-start

commit v3 on v2

--- a/solution.py
+++ b/solution.py
@@ -266,57 +266,45 @@
             self.keep.wait()
 
 
-class Parts:
-    def __init__(self, y0, core0, src, window, out, send, recv):
-        y, core, _, z = place()
-        self.owner = (y == y0) & (core == core0)
-        self.relay = (y != y0) & (core == core0)
-        self.leaf = core != core0
-        self.src, self.window, self.out, self.send, self.recv, self.y, self.core, self.z = src, window, out, send, recv, y, core, z
-
-    def rows(self, dist):
-        return pl.ds(pl.multiple_of((self.z + NZ - dist) % NZ * 8, 8), 8)
-
-    def copy(self, dist, dy, passed=False):
-        rows = self.rows(dist)
-        dst = self.out.at[:, rows]
-        src = dst if passed else self.src.at[:, rows, self.window]
-        peer = (self.y + dy) % NY * 2 + self.core if dy else self.y * 2 + 1 - self.core
-        return remote(src, dst, self.send.at[dist, dy], self.recv.at[dist], {"prow": peer})
-
-    def start(self, dist):
-        @pl.when(self.owner)
-        def _():
-            for dy in (1, 3, 2, 0):
-                self.copy(dist, dy).start()
-
-    def forward(self, dist):
-        @pl.when(self.relay)
-        def _():
-            self.copy(dist, 0, True).wait_recv()
-            self.copy(dist, 0, True).start()
+class DirectSum:
+    def __init__(self, s, out, parts, send, recv):
+        y, core, _, _ = place()
+        self.s, self.out, self.parts, self.send, self.recv = s, out, parts, send, recv
+        self.prow = y * 2 + core
+        self.q = s.shape[0] // 8
+
+    def rows(self, d):
+        return pl.ds(pl.multiple_of((self.prow + d) % 8 * self.q, self.q), self.q)
+
+    def scatter(self, d):
+        peer = {"prow": (self.prow + d) % 8}
+        return remote(self.s.at[self.rows(d)], self.parts.at[d], self.send.at[0, d], self.recv.at[0, d], peer)
+
+    def spread(self, d):
+        mine = self.out.at[self.rows(0)]
+        return remote(mine, mine, self.send.at[1, d], self.recv.at[1, d], {"prow": (self.prow + d) % 8})
+
+    def start(self):
+        for d in range(1, 8):
+            self.scatter(d).start()
+
+    def total(self):
+        total = self.s[self.rows(0), :]
+        for d in range(1, 8):
+            self.scatter(d).wait_recv()
+            total = total + self.parts[d]
+        self.out[self.rows(0), :] = total
+        for d in range(1, 8):
+            self.spread(d).start()
 
     def finish(self):
-        @pl.when(self.owner)
-        def _():
-            self.out[...] = self.src[:, :, self.window]
-
-        @pl.when(self.leaf)
-        def _():
-            for dist in range(NZ):
-                self.copy(dist, 0, True).wait_recv()
+        for d in range(1, 8):
+            self.spread(d).wait_recv()
 
     def flush(self):
-        @pl.when(self.owner)
-        def _():
-            for dist in range(NZ):
-                for dy in range(NY):
-                    self.copy(dist, dy).wait_send()
-
-        @pl.when(self.relay)
-        def _():
-            for dist in range(NZ):
-                self.copy(dist, 0, True).wait_send()
+        for d in range(1, 8):
+            self.scatter(d).wait_send()
+            self.spread(d).wait_send()
 
 
 class Sum:
@@ -399,10 +387,8 @@
     a_lo,
     ae,
     gram,
-    gtop,
-    ghalf,
-    gquarter,
-    gacc,
+    gfull,
+    gparts,
     aps,
     apt,
     ahalf,
@@ -410,6 +396,7 @@
     aacc,
     av,
     avt,
+    xct,
     linv_s,
     t_s,
     vct_s,
@@ -490,87 +477,61 @@
     top = Broadcast(0, 0, a_ref.at[pl.ds(0, nb)], ae, esend, erecv)
     top.start()
     window = pl.ds(pl.multiple_of(pcol % 4 * cols, cols), cols)
-    part = Parts(x, z // 4, pt_ref, window, pct, psend, precv)
+    part = Broadcast(x, z // 4, pt_ref.at[:, :, window], pct, psend, precv)
 
     def split_a():
         load.wait()
         a_hi[...], a_lo[...] = split(a_buf[...])
-
-    def step(i):
-        def run():
-            part.start(((0,) + ORDER)[i])
-            if i:
-                part.forward(((0,) + ORDER)[i - 1])
-            if i == 1:
-                split_a()
-            if i == 4:
-                top.forward()
-
-        return run
 
     panel_flush = gather(
         lambda xx, zz: pt_ref.at[xx, pl.ds(pl.multiple_of(zz * 8, 8), 8)],
         panel_send,
         panel_recv,
-        [step(i) for i in range(7)],
+        (lambda: None, split_a),
     )
-    part.start(ORDER[6])
-    part.forward(ORDER[5])
+    top.forward()
     panel = pt_ref[...].reshape(nb, wide)
     gram[...] = mm(panel, panel, NT)
 
-    gsum = Sum(gram, gtop, ghalf, gquarter, gacc, gsend, grecv)
+    gsum = DirectSum(gram, gfull, gparts, gsend, grecv)
     asum = Sum(aps, apt, ahalf, aquarter, aacc, asend, arecv)
-    gsum.exchange()
+    gsum.start()
     handed = []
     for r in range(1, 8):
-        piece = pl.ds(r % 2 * h + r // 2 * q, q)
-        src = pt_ref.at[(r % 2 * h + r // 2 * q) // 64, pl.ds((r % 2 * h + r // 2 * q) % 64, q), pl.ds(0, nb)]
-        dst = gtop.at[piece, pl.ds(nb, nb)]
-        handed.append(remote(src, dst, hsend.at[r], hrecv.at[0], {"prow": r}))
+        start = r % 2 * h + r // 2 * q
+        src = pt_ref.at[start // 64, pl.ds(start % 64, q), pl.ds(0, nb)]
+        handed.append(remote(src, apt.at[pl.ds(start, q), pl.ds(cols, nb)], hsend.at[r], hrecv.at[0], {"prow": r}))
+
+    aps[...] = mm3(split(panel), (a_hi[...], a_lo[...]))
+    asum.exchange()
+    gsum.total()
 
     @pl.when(prow == 0)
     def _():
         for copy in handed:
             copy.start()
-        gtop[pl.ds(0, q), pl.ds(nb, nb)] = pt_ref[0, pl.ds(0, q), pl.ds(0, nb)]
-
-    def product(half):
-        mine = pt_ref[pl.ds(half * 2, 2)].reshape(h, wide)
-        aps[gsum.rows(half * h, h), :] = mm3(split(mine), (a_hi[...], a_lo[...]))
-
-    product(1 - core)
-    asum.exchange()
-    gsum.quarters()
-    product(core)
-    gsum.total()
-
-    @pl.when(prow != 0)
-    def _():
-        piece = gtop.at[gsum.own, pl.ds(nb, nb)]
-        remote(piece, piece, hsend.at[0], hrecv.at[0], gsum.mate).wait_recv()
-
-    gsum.spread()
+        apt[pl.ds(0, q), pl.ds(cols, nb)] = pt_ref[0, pl.ds(0, q), pl.ds(0, nb)]
+
     asum.quarters()
-    gsum.forward()
+    part.start()
     gsum.finish()
 
     def first():
         asum.total()
+
+        @pl.when(prow != 0)
+        def _():
+            piece = apt.at[asum.own, pl.ds(cols, nb)]
+            remote(piece, piece, hsend.at[0], hrecv.at[0], asum.mate).wait_recv()
+
         asum.spread()
 
-    def second():
-        asum.forward()
-        part.forward(ORDER[6])
-
-    def third():
-        asum.finish()
-        part.finish()
-
-    stages = iter([first, second, third, top.finish])
-    linv = lower_inverse(gtop[:, 0:nb], lambda: next(stages)())
+    stages = iter([first, asum.forward, lambda: None, part.forward])
+    linv = lower_inverse(gfull[...], lambda: next(stages)())
     linv_s[...] = linv
-    avt[...] = mm(linv, apt[...]) - ae[...]
+    asum.finish()
+    top.finish()
+    avt[...] = mm(linv, apt[:, 0:cols]) - ae[...]
     av[...] = avt[...].T
 
     mine = pl.ds(pl.multiple_of(prow * rows, rows), rows)
@@ -585,10 +546,6 @@
     @pl.when(stays)
     def _():
         out_ref[pl.ds(pl.multiple_of(pcol * rows, rows), rows), :] = av[mine, :]
-
-    @pl.when(moves)
-    def _():
-        swap.wait_recv()
 
     def along_x(src, dst, sends, recvs, dx):
         return remote(src, dst, sends.at[dx], recvs.at[dx], {"pcol": (x + dx) % NX * NZ + z})
@@ -603,9 +560,9 @@
 
     def factor_first():
         linv = linv_s[...]
-        side = mm(linv, gtop[:, nb:])
+        side = mm(linv, apt[:, cols:])
         r, c = iota((nb, nb), 0), iota((nb, nb), 1)
-        ygram = 2.0 * (r == c).astype(F32) - side - mm(gtop[:, nb:], linv, ((0,), (1,)))
+        ygram = 2.0 * (r == c).astype(F32) - side - mm(apt[:, cols:], linv, ((0,), (1,)))
         t_s[...] = jnp.where(r < c, ygram, jnp.where(r == c, 0.5 * ygram, 0.0))
 
     def factor_second():
@@ -654,33 +611,40 @@
             remote(m_rows, m_rows, wsend.at[d], wrecv.at[d], {"prow": (prow + d) % 8}).wait_recv()
         t, vct, linv = t_s[...], vct_s[...], linv_s[...]
         k = mm(t, mm(mraw[...], t), TN)
-        b = mm(t, avt[...], TN) - mm(0.5 * (k + k.T), vct)
+        b = xct[...] - mm(0.5 * (k + k.T), vct)
         b_ref[...] = b
         c_ref[...] = mm(linv, b, TN)
-        d_ref[...] = mm(t, vct)
         sel = (iota((8, nb), 1) == iota((8, nb), 0) + 8 * pcol).astype(F32)
         kt = mm(sel, k, NT)
         l_ref[0:8, :] = kt
         l_ref[8:16, :] = mm(kt, linv)
         l_ref[16:24, :] = mm(sel, t, NT)
 
-    def fourth():
-        merge(BASE)
-        m_second()
-
-    def fifth():
-        merge(2 * BASE)
-        m_third()
+    def ready():
+        t = t_s[...]
+        xct[...] = mm(t, avt[...], TN)
+        d_ref[...] = mm(t, vct_s[...])
+
+    factor_first()
+    factor_second()
+    merge(BASE)
+    merge(2 * BASE)
+    part.finish()
+    m_first()
+
+    @pl.when(moves)
+    def _():
+        swap.wait_recv()
 
     flush = gather(
         lambda xx, zz: out_ref.at[pl.ds(pl.multiple_of((xx * NZ + zz) * rows, rows), rows)],
         send,
         recv,
-        (m_first, factor_first, factor_second, fourth, fifth, m_fourth, last),
+        (ready, m_second, lambda: None, m_third, lambda: None, m_fourth),
     )
+    last()
     flush()
     panel_flush()
-    part.flush()
 
     gsum.flush()
     asum.flush()
@@ -756,16 +720,15 @@
             pltpu.VMEM((rows, cols), jnp.bfloat16),
             buf(nb, cols),
             buf(nb, nb),
-            buf(nb, 2 * nb),
-            buf(h, nb),
-            buf(NY, q, nb),
-            buf(h, nb),
+            buf(nb, nb),
+            buf(8, q, nb),
             buf(nb, cols),
-            buf(nb, cols),
+            buf(nb, cols + nb),
             buf(h, cols),
             buf(NY, q, cols),
             buf(h, cols),
             buf(cols, nb),
+            buf(nb, cols),
             buf(nb, cols),
             buf(nb, nb),
             buf(nb, nb),
@@ -781,14 +744,14 @@
             dma((NX, NZ)),
             dma((NY + 1,)),
             dma((1,)),
-            dma((11,)),
-            dma((11,)),
+            dma((2, 8)),
+            dma((2, 8)),
             dma((8,)),
             dma((1,)),
             dma((11,)),
             dma((11,)),
-            dma((NZ, NY)),
-            dma((NZ,)),
+            dma((NY + 1,)),
+            dma((1,)),
             dma((2,)),
             dma((NX, NZ)),
             dma((NX, NZ)),

time: 130 us -> 125 us (0.962)
  Pallas kernels: 128 us -> 123 us
    pallas_call x1, Pallas kernels: 121 us -> 116 us  [shards(): pl.pallas_call(main_kernel, out_shape=(shape(NX, nb // NX, rows), shape(r...]
where the time goes in v3:
time: 125 us
  Pallas kernels  123 us (98%)
    pallas_call x1, Pallas kernels, shards(): pl.pallas_call(main_kernel, out_shape=(shape(NX, nb // NX, rows), shape(r...  116 us
    pallas_call x1, Pallas kernels, shards(): pl.pallas_call(update_kernel, grid=(rows // tile,), out_shape=(shape(rows...  7.9 us

profile of v3, /device:TPU:1, one launch (start us, length us, event | category | flops | bytes accessed | tf_op | source)
XLA Modules:
  0.0 124.9 jit_solution(18056534620722433792)
XLA Ops:
  0.6 0.0 copy-start
  0.6 0.8 copy-done
  1.5 115.6 %shard_map.41 = (f32[4,64,2048]{2,1,0:T(8,128)S(1)}, f32[2048,256]{1,0:T(8,128)S(1)}, f32[256,512]{1,0:T(8,128)S(1)}, f32[256,512]{1,0:T(8,128)S(1)}, f32[256,512]{1,0:T(8,128)S(1)}, /*index=5*/f32[24,256]{1,0:T(8,128)S(1)}) custom-call(f32[8,2048]{1,0:T(8,128)S(1)} %bitcast.4, f32[2048,512]{1,0:T(8,128)} %a_ref.3), custom_call_target="tpu_custom_call" | custom-call | tf_op jit(solution)/shard_map/pallas_call | solution.py:712
  117.0 7.9 %shard_map.42 = (f32[2048,512]{1,0:T(8,128)}, f32[8,2048]{1,0:T(8,128)}) custom-call(f32[2048,512]{1,0:T(8,128)} %a_ref.3, f32[256,2048]{1,0:T(8,128)S(1)} %bitcast.3, f32[2048,256]{1,0:T(8,128)S(1)} %get-tuple-element.11.av_ref, f32[256,512]{1,0:T(8,128)S(1)} %get-tuple-element.12.c_ref, f32[256,512]{1,0:T(8,128)S(1)} %get-tuple-element.13.d_ref, ...), custom_call_target="tpu_custom_call" | custom-call | tf_op jit(solution)/shard_map/pallas_call | solution.py:772
Async XLA Ops:
  0.6 0.8 copy-start

commit v4 on v3

--- a/solution.py
+++ b/solution.py
@@ -144,7 +144,7 @@
 ORDER = (1, 7, 2, 6, 3, 5, 4)
 
 
-def gather(at, send, recv, hooks=()):
+def gather(at, send, recv, before=None, hooks=()):
     _, core, x, z = place()
 
     def slab(xx, zz):
@@ -182,6 +182,12 @@
             along_x(dx, 0).start()
         along_z(0, 1).start()
         along_z(0, NZ - 1).start()
+
+    if before:
+        before()
+
+    @pl.when(core == 1)
+    def _():
         for dx in range(1, NX):
             arrived(dx, 0)
             along_z(dx, 1).start()
@@ -225,43 +231,65 @@
 class Broadcast:
     def __init__(self, y0, core0, src, out, send, recv):
         y, core, _, _ = place()
-        self.owner = (y == y0) & (core == core0)
-        self.relay = (y != y0) & (core == core0)
+        away = (y + NY - y0) % NY
+        self.owner = (away == 0) & (core == core0)
+        self.next = (away == 1) & (core == core0)
+        self.last = (away == 3) & (core == core0)
+        self.far_one = (away == 2) & (core == core0)
+        self.relay = (away != 0) & (core == core0)
         self.leaf = core != core0
-        self.along = [
-            remote(src, out, send.at[dy], recv.at[0], {"prow": (y + dy) % NY * 2 + core}) for dy in range(1, NY)
-        ]
-        self.own = remote(src, out, send.at[0], recv.at[0], {"prow": y * 2 + 1 - core})
-        self.pass_on = remote(out, out, send.at[0], recv.at[0], {"prow": y * 2 + 1 - core})
-        self.keep = pltpu.make_async_copy(src, out, send.at[NY])
+        mate = {"prow": y * 2 + 1 - core}
+        up, down = {"prow": (y + 1) % NY * 2 + core}, {"prow": (y + 3) % NY * 2 + core}
+        self.up = remote(src, out, send.at[1], recv.at[0], up)
+        self.down = remote(src, out, send.at[2], recv.at[0], down)
+        self.own = remote(src, out, send.at[0], recv.at[0], mate)
+        self.on = remote(out, out, send.at[1], recv.at[0], up)
+        self.pass_on = remote(out, out, send.at[0], recv.at[0], mate)
+        self.keep = pltpu.make_async_copy(src, out, send.at[3])
 
     def start(self):
         @pl.when(self.owner)
         def _():
-            for copy in self.along:
-                copy.start()
+            self.up.start()
+            self.down.start()
             self.own.start()
             self.keep.start()
 
-    def forward(self):
-        @pl.when(self.relay)
+    def near(self):
+        @pl.when(self.next)
+        def _():
+            self.on.wait_recv()
+            self.on.start()
+            self.pass_on.start()
+
+        @pl.when(self.last)
         def _():
             self.pass_on.wait_recv()
             self.pass_on.start()
 
+    def far(self):
+        @pl.when(self.far_one)
+        def _():
+            self.pass_on.wait_recv()
+            self.pass_on.start()
+
     def finish(self):
         @pl.when(self.relay)
         def _():
             self.pass_on.wait_send()
 
+        @pl.when(self.next)
+        def _():
+            self.on.wait_send()
+
         @pl.when(self.leaf)
         def _():
             self.pass_on.wait_recv()
 
         @pl.when(self.owner)
         def _():
-            for copy in self.along:
-                copy.wait_send()
+            self.up.wait_send()
+            self.down.wait_send()
             self.own.wait_send()
             self.keep.wait()
 
@@ -293,7 +321,9 @@
         for d in range(1, 8):
             self.scatter(d).wait_recv()
             total = total + self.parts[d]
-        self.out[self.rows(0), :] = total
+        return total
+
+    def share(self):
         for d in range(1, 8):
             self.spread(d).start()
 
@@ -386,6 +416,9 @@
     a_hi,
     a_lo,
     ae,
+    aet,
+    ae64,
+    ap64,
     gram,
     gfull,
     gparts,
@@ -394,14 +427,13 @@
     ahalf,
     aquarter,
     aacc,
-    av,
-    avt,
-    xct,
+    ptop,
+    pct,
     linv_s,
     t_s,
-    vct_s,
-    pct,
     mpart,
+    mparts,
+    mq,
     mx,
     mz,
     mown,
@@ -419,7 +451,10 @@
     arecv,
     psend,
     precv,
-    fsem,
+    fsend,
+    frecv,
+    ksend,
+    krecv,
     send,
     recv,
     xsend,
@@ -435,19 +470,19 @@
     prow, pcol = y * 2 + core, x * NZ + z
     nb = out_ref.shape[1]
     cols = ae.shape[1]
-    h, q = nb // 2, nb // 8
     rows = cols // 8
+    q = nb // 8
     wide = slab_ref.shape[1]
 
     load = pltpu.make_async_copy(a_ref, a_buf, acopy.at[0])
     load.start()
 
-    to_row, to_col = pcol // 4, pcol % 4 * 8 + prow
-    from_col, from_row = prow * 4 + pcol // 8, pcol % 8
+    to_row, to_col = pcol // 4, pcol % 4 * 8 + core * NY + y
+    source_col, j = prow * 4 + pcol // 8, pcol % 8
     stays = (to_row == prow) & (to_col == pcol)
     moves = jnp.logical_not(stays)
-    target = {"prow": to_row, "pcol": to_col}
-    source = {"prow": from_row, "pcol": from_col}
+    corner = (prow == 0) & (pcol == 0)
+    source = {"prow": j % NY * 2 + j // NY, "pcol": source_col}
     barrier = pltpu.get_barrier_semaphore()
     peers = [{"prow": (prow + d) % 8} for d in range(1, 8)]
     peers += [{"pcol": (x + dx) % NX * NZ + z} for dx in range(1, NX)]
@@ -461,108 +496,151 @@
 
     @pl.when(moves)
     def _():
-        greet(target)
         greet(source)
 
+    @pl.when(jnp.logical_not(corner))
+    def _():
+        greet({"prow": 0, "pcol": source_col})
+
     pt_ref[x, pl.ds(pl.multiple_of(z * 8, 8), 8), :] = slab_ref[...]
-
-    @pl.when(moves)
-    def _():
-        pl.semaphore_wait(barrier, len(peers) + 2)
-
-    @pl.when(stays)
-    def _():
-        pl.semaphore_wait(barrier, len(peers))
+    extra = jnp.where(moves, 1, 0) + jnp.where(prow == 0, 8, 0) - jnp.where(corner, 1, 0)
+    pl.semaphore_wait(barrier, len(peers) + extra)
 
     top = Broadcast(0, 0, a_ref.at[pl.ds(0, nb)], ae, esend, erecv)
-    top.start()
     window = pl.ds(pl.multiple_of(pcol % 4 * cols, cols), cols)
     part = Broadcast(x, z // 4, pt_ref.at[:, :, window], pct, psend, precv)
-
-    def split_a():
+    head = Broadcast(0, 0, pt_ref.at[:, :, pl.ds(0, nb)], ptop, hsend, hrecv)
+
+    def top_piece(k):
+        peer = {"prow": pcol // 4, "pcol": pcol % 4 * 8 + k}
+        return remote(aet.at[pl.ds(k * rows, rows)], ae64, ksend.at[k], krecv.at[0], peer)
+
+    def take_a():
         load.wait()
         a_hi[...], a_lo[...] = split(a_buf[...])
+
+        @pl.when(prow == 0)
+        def _():
+            aet[...] = a_buf[0:nb, :].T
+            for k in range(1, 8):
+                top_piece(k).start()
+
+        @pl.when((prow == 0) & (pcol != 0))
+        def _():
+            top_piece(0).start()
+
+        @pl.when(corner)
+        def _():
+            ae64[...] = aet[0:rows, :]
 
     panel_flush = gather(
         lambda xx, zz: pt_ref.at[xx, pl.ds(pl.multiple_of(zz * 8, 8), 8)],
         panel_send,
         panel_recv,
-        (lambda: None, split_a),
+        top.start,
+        (lambda: None, take_a),
     )
-    top.forward()
     panel = pt_ref[...].reshape(nb, wide)
     gram[...] = mm(panel, panel, NT)
 
     gsum = DirectSum(gram, gfull, gparts, gsend, grecv)
     asum = Sum(aps, apt, ahalf, aquarter, aacc, asend, arecv)
+    msum = DirectSum(mpart, mraw, mparts, wsend, wrecv)
     gsum.start()
-    handed = []
-    for r in range(1, 8):
-        start = r % 2 * h + r // 2 * q
-        src = pt_ref.at[start // 64, pl.ds(start % 64, q), pl.ds(0, nb)]
-        handed.append(remote(src, apt.at[pl.ds(start, q), pl.ds(cols, nb)], hsend.at[r], hrecv.at[0], {"prow": r}))
-
-    aps[...] = mm3(split(panel), (a_hi[...], a_lo[...]))
+    aps[...] = mm3(split(panel), (a_hi[...], a_lo[...])).T
     asum.exchange()
-    gsum.total()
-
-    @pl.when(prow == 0)
-    def _():
-        for copy in handed:
-            copy.start()
-        apt[pl.ds(0, q), pl.ds(cols, nb)] = pt_ref[0, pl.ds(0, q), pl.ds(0, nb)]
-
+    gfull[gsum.rows(0), :] = gsum.total()
+    gsum.share()
     asum.quarters()
-    part.start()
+    head.start()
     gsum.finish()
 
-    def first():
+    swap = remote(apt.at[asum.own], ap64, fsend.at[0], frecv.at[0], {"prow": to_row, "pcol": to_col})
+
+    def hand_on():
         asum.total()
 
-        @pl.when(prow != 0)
-        def _():
-            piece = apt.at[asum.own, pl.ds(cols, nb)]
-            remote(piece, piece, hsend.at[0], hrecv.at[0], asum.mate).wait_recv()
-
-        asum.spread()
-
-    stages = iter([first, asum.forward, lambda: None, part.forward])
+        @pl.when(moves)
+        def _():
+            swap.start()
+
+        @pl.when(stays)
+        def _():
+            ap64[...] = apt[asum.own, :]
+
+    def relay():
+        head.far()
+        top.near()
+
+    stages = iter([hand_on, head.near, relay, lambda: None])
     linv = lower_inverse(gfull[...], lambda: next(stages)())
     linv_s[...] = linv
-    asum.finish()
-    top.finish()
-    avt[...] = mm(linv, apt[:, 0:cols]) - ae[...]
-    av[...] = avt[...].T
-
-    mine = pl.ds(pl.multiple_of(prow * rows, rows), rows)
-    swap = remote(
-        av.at[mine], out_ref.at[pl.ds(pl.multiple_of(to_col * rows, rows), rows)], fsem.at[0], fsem.at[1], target
-    )
 
     @pl.when(moves)
     def _():
-        swap.start()
-
-    @pl.when(stays)
-    def _():
-        out_ref[pl.ds(pl.multiple_of(pcol * rows, rows), rows), :] = av[mine, :]
+        swap.wait_recv()
+
+    @pl.when(jnp.logical_not(corner))
+    def _():
+        top_piece(0).wait_recv()
+
+    out_ref[pl.ds(pl.multiple_of(pcol * rows, rows), rows), :] = mm(ap64[...], linv, NT) - ae64[...]
 
     def along_x(src, dst, sends, recvs, dx):
         return remote(src, dst, sends.at[dx], recvs.at[dx], {"pcol": (x + dx) % NX * NZ + z})
 
-    def m_first():
-        e = (iota((nb, cols), 0) == iota((nb, cols), 1)) & (pcol == 0)
-        vct_s[...] = mm(linv_s[...], pct[...].reshape(nb, cols)) - e.astype(F32)
-        mpart[...] = mm(vct_s[pl.ds(pl.multiple_of(prow * q, q), q), :], av[...])
+    def along_z(dz):
+        return remote(mown, mz.at[dz], zsend.at[dz], zrecv.at[dz], {"pcol": x * NZ + (z + dz) % NZ})
+
+    def m_scatter():
+        lanes = 2 * rows
+        block = pcol // 2 * lanes
+        p = pt_ref[:, :, pl.ds(pl.multiple_of(block, lanes), lanes)].reshape(nb, lanes)
+        row, lane = iota((nb, lanes), 0), iota((nb, lanes), 1)
+        v = mm(linv_s[...], p) - (row == lane + block + prow * wide).astype(F32)
+        v = jnp.where(lane // rows == pcol % 2, v, 0.0)
+        av = out_ref[pl.ds(pl.multiple_of(pcol * rows, rows), rows), :]
+        mpart[...] = mm(v, jnp.concatenate([av, av], 0))
+        msum.start()
+
+    def m_x():
+        mq[...] = msum.total()
         for dx in range(1, NX):
             piece = pl.ds(pl.multiple_of((x + dx) % NX * 8, 8), 8)
-            along_x(mpart.at[piece], mx.at[dx], xsend, xrecv, dx).start()
+            along_x(mq.at[piece], mx.at[dx], xsend, xrecv, dx).start()
+
+    def m_z():
+        total = mq[pl.ds(pl.multiple_of(x * 8, 8), 8), :]
+        for dx in range(1, NX):
+            along_x(mx.at[dx], mx.at[dx], xsend, xrecv, dx).wait_recv()
+            total = total + mx[dx]
+        mown[...] = total
+        for dz in range(1, NZ):
+            along_z(dz).start()
+
+    m_rows = pl.ds(pl.multiple_of(prow * q + x * 8, 8), 8)
+    m_own = mraw.at[m_rows]
+
+    def m_back():
+        total = mown[...]
+        for dz in range(1, NZ):
+            along_z(dz).wait_recv()
+            total = total + mz[dz]
+        mraw[m_rows, :] = total
+        for dx in range(1, NX):
+            along_x(m_own, m_own, xgsend, xgrecv, dx).start()
+
+    def m_share():
+        for dx in range(1, NX):
+            along_x(m_own, m_own, xgsend, xgrecv, dx).wait_recv()
+        msum.share()
 
     def factor_first():
         linv = linv_s[...]
-        side = mm(linv, apt[:, cols:])
+        first = ptop[...].reshape(nb, nb)
+        side = mm(linv, first)
         r, c = iota((nb, nb), 0), iota((nb, nb), 1)
-        ygram = 2.0 * (r == c).astype(F32) - side - mm(apt[:, cols:], linv, ((0,), (1,)))
+        ygram = 2.0 * (r == c).astype(F32) - side - mm(first, linv, ((0,), (1,)))
         t_s[...] = jnp.where(r < c, ygram, jnp.where(r == c, 0.5 * ygram, 0.0))
 
     def factor_second():
@@ -579,92 +657,80 @@
         for lo, hi, side in sides:
             t_s[lo, hi] = side
 
-    def m_second():
-        total = mpart[pl.ds(pl.multiple_of(x * 8, 8), 8), :]
-        for dx in range(1, NX):
-            along_x(mx.at[dx], mx.at[dx], xsend, xrecv, dx).wait_recv()
-            total = total + mx[dx]
-        mown[...] = total
-        for dz in range(1, NZ):
-            remote(mown, mz.at[dz], zsend.at[dz], zrecv.at[dz], {"pcol": x * NZ + (z + dz) % NZ}).start()
-
-    m_own = mraw.at[pl.ds(pl.multiple_of(prow * q + x * 8, 8), 8)]
-    m_rows = mraw.at[pl.ds(pl.multiple_of(prow * q, q), q)]
-
-    def m_third():
-        total = mown[...]
-        for dz in range(1, NZ):
-            remote(mown, mz.at[dz], zsend.at[dz], zrecv.at[dz], {"pcol": x * NZ + (z + dz) % NZ}).wait_recv()
-            total = total + mz[dz]
-        mraw[pl.ds(pl.multiple_of(prow * q + x * 8, 8), 8), :] = total
-        for dx in range(1, NX):
-            along_x(m_own, m_own, xgsend, xgrecv, dx).start()
-
-    def m_fourth():
-        for dx in range(1, NX):
-            along_x(m_own, m_own, xgsend, xgrecv, dx).wait_recv()
-        for d in range(1, 8):
-            remote(m_rows, m_rows, wsend.at[d], wrecv.at[d], {"prow": (prow + d) % 8}).start()
-
-    def last():
-        for d in range(1, 8):
-            remote(m_rows, m_rows, wsend.at[d], wrecv.at[d], {"prow": (prow + d) % 8}).wait_recv()
-        t, vct, linv = t_s[...], vct_s[...], linv_s[...]
-        k = mm(t, mm(mraw[...], t), TN)
-        b = xct[...] - mm(0.5 * (k + k.T), vct)
-        b_ref[...] = b
-        c_ref[...] = mm(linv, b, TN)
-        sel = (iota((8, nb), 1) == iota((8, nb), 0) + 8 * pcol).astype(F32)
-        kt = mm(sel, k, NT)
-        l_ref[0:8, :] = kt
-        l_ref[8:16, :] = mm(kt, linv)
-        l_ref[16:24, :] = mm(sel, t, NT)
-
-    def ready():
-        t = t_s[...]
-        xct[...] = mm(t, avt[...], TN)
-        d_ref[...] = mm(t, vct_s[...])
-
-    factor_first()
-    factor_second()
-    merge(BASE)
-    merge(2 * BASE)
-    part.finish()
-    m_first()
-
-    @pl.when(moves)
-    def _():
-        swap.wait_recv()
+    def before():
+        asum.spread()
+        part.start()
+        m_scatter()
+        head.finish()
+
+    def first():
+        factor_first()
+        top.far()
+
+    def second():
+        m_x()
+        asum.forward()
+
+    def fourth():
+        m_z()
+        part.near()
+
+    def fifth():
+        merge(BASE)
+        merge(2 * BASE)
+        part.far()
 
     flush = gather(
         lambda xx, zz: out_ref.at[pl.ds(pl.multiple_of((xx * NZ + zz) * rows, rows), rows)],
         send,
         recv,
-        (ready, m_second, lambda: None, m_third, lambda: None, m_fourth),
+        before,
+        (first, second, factor_second, fourth, fifth, m_back, m_share),
     )
-    last()
+
+    asum.finish()
+    top.finish()
+    part.finish()
+    linv, t = linv_s[...], t_s[...]
+    e = (iota((nb, cols), 0) == iota((nb, cols), 1)) & (pcol == 0)
+    vct = mm(linv, pct[...].reshape(nb, cols)) - e.astype(F32)
+    xc = mm(t, mm(linv, apt[...], NT) - ae[...], TN)
+    d_ref[...] = mm(t, vct)
+    msum.finish()
+    k = mm(t, mm(mraw[...], t), TN)
+    b = xc - mm(0.5 * (k + k.T), vct)
+    b_ref[...] = b
+    c_ref[...] = mm(linv, b, TN)
+    sel = (iota((8, nb), 1) == iota((8, nb), 0) + 8 * pcol).astype(F32)
+    kt = mm(sel, k, NT)
+    l_ref[0:8, :] = kt
+    l_ref[8:16, :] = mm(kt, linv)
+    l_ref[16:24, :] = mm(sel, t, NT)
+
     flush()
     panel_flush()
-
     gsum.flush()
     asum.flush()
+    msum.flush()
 
     @pl.when(prow == 0)
     def _():
-        for copy in handed:
-            copy.wait_send()
+        for k in range(1, 8):
+            top_piece(k).wait_send()
+
+    @pl.when((prow == 0) & (pcol != 0))
+    def _():
+        top_piece(0).wait_send()
 
     @pl.when(moves)
     def _():
         swap.wait_send()
 
     for dx in range(1, NX):
-        along_x(mpart.at[pl.ds(0, 8)], mx.at[dx], xsend, xrecv, dx).wait_send()
+        along_x(mq.at[pl.ds(0, 8)], mx.at[dx], xsend, xrecv, dx).wait_send()
         along_x(m_own, m_own, xgsend, xgrecv, dx).wait_send()
     for dz in range(1, NZ):
-        remote(mown, mz.at[dz], zsend.at[dz], zrecv.at[dz], {"pcol": x * NZ + (z + dz) % NZ}).wait_send()
-    for d in range(1, 8):
-        remote(m_rows, m_rows, wsend.at[d], wrecv.at[d], {"prow": (prow + d) % 8}).wait_send()
+        along_z(dz).wait_send()
 
 
 def params(cid):
@@ -708,7 +774,7 @@
     dma = pltpu.SemaphoreType.DMA
     buf = lambda *dims: pltpu.VMEM(dims, F32)
 
-    h, q = nb // 2, nb // 8
+    q = nb // 8
     pt, av, c, d, b, l = pl.pallas_call(
         main_kernel,
         out_shape=(shape(NX, nb // NX, rows), shape(rows, nb)) + (shape(nb, cols),) * 3 + (shape(24, nb),),
@@ -719,21 +785,23 @@
             pltpu.VMEM((rows, cols), jnp.bfloat16),
             pltpu.VMEM((rows, cols), jnp.bfloat16),
             buf(nb, cols),
+            buf(cols, nb),
+            buf(cols // 8, nb),
+            buf(cols // 8, nb),
             buf(nb, nb),
             buf(nb, nb),
             buf(8, q, nb),
-            buf(nb, cols),
-            buf(nb, cols + nb),
-            buf(h, cols),
-            buf(NY, q, cols),
-            buf(h, cols),
             buf(cols, nb),
-            buf(nb, cols),
-            buf(nb, cols),
+            buf(cols, nb),
+            buf(cols // 2, nb),
+            buf(NY, cols // 8, nb),
+            buf(cols // 2, nb),
+            buf(NX, nb // NX, nb),
+            buf(NX, nb // NX, cols),
             buf(nb, nb),
             buf(nb, nb),
-            buf(nb, cols),
-            buf(NX, nb // NX, cols),
+            buf(nb, nb),
+            buf(8, q, nb),
             buf(q, nb),
             buf(NX, 8, nb),
             buf(NZ, 8, nb),
@@ -742,17 +810,20 @@
             dma((1,)),
             dma((NX, NZ)),
             dma((NX, NZ)),
-            dma((NY + 1,)),
+            dma((4,)),
             dma((1,)),
             dma((2, 8)),
             dma((2, 8)),
-            dma((8,)),
+            dma((4,)),
             dma((1,)),
             dma((11,)),
             dma((11,)),
-            dma((NY + 1,)),
+            dma((4,)),
             dma((1,)),
-            dma((2,)),
+            dma((1,)),
+            dma((1,)),
+            dma((8,)),
+            dma((1,)),
             dma((NX, NZ)),
             dma((NX, NZ)),
             dma((NX,)),
@@ -761,8 +832,8 @@
             dma((NZ,)),
             dma((NX,)),
             dma((NX,)),
-            dma((8,)),
-            dma((8,)),
+            dma((2, 8)),
+            dma((2, 8)),
         ],
         compiler_params=params(2),
     )(pt_own, trailing)

time: 125 us -> 122 us (0.976)
  Pallas kernels: 123 us -> 120 us
    pallas_call x1, Pallas kernels: 116 us -> 112 us  [shards(): pl.pallas_call(main_kernel, out_shape=(shape(NX, nb // NX, rows), shape(r...]
where the time goes in v4:
time: 122 us
  Pallas kernels  120 us (98%)
    pallas_call x1, Pallas kernels, shards(): pl.pallas_call(main_kernel, out_shape=(shape(NX, nb // NX, rows), shape(r...  112 us
    pallas_call x1, Pallas kernels, shards(): pl.pallas_call(update_kernel, grid=(rows // tile,), out_shape=(shape(rows...  7.9 us

profile of v4, /device:TPU:1, one launch (start us, length us, event | category | flops | bytes accessed | tf_op | source)
XLA Modules:
  0.0 121.6 jit_solution(2746726944650384358)
XLA Ops:
  0.6 0.0 copy-start
  0.6 0.8 copy-done
  1.5 112.2 %shard_map.41 = (f32[4,64,2048]{2,1,0:T(8,128)S(1)}, f32[2048,256]{1,0:T(8,128)S(1)}, f32[256,512]{1,0:T(8,128)S(1)}, f32[256,512]{1,0:T(8,128)S(1)}, f32[256,512]{1,0:T(8,128)S(1)}, /*index=5*/f32[24,256]{1,0:T(8,128)S(1)}) custom-call(f32[8,2048]{1,0:T(8,128)S(1)} %bitcast.4, f32[2048,512]{1,0:T(8,128)} %a_ref.3), custom_call_target="tpu_custom_call" | custom-call | tf_op jit(solution)/shard_map/pallas_call | solution.py:778
  113.6 7.9 %shard_map.42 = (f32[2048,512]{1,0:T(8,128)}, f32[8,2048]{1,0:T(8,128)}) custom-call(f32[2048,512]{1,0:T(8,128)} %a_ref.3, f32[256,2048]{1,0:T(8,128)S(1)} %bitcast.3, f32[2048,256]{1,0:T(8,128)S(1)} %get-tuple-element.11.av_ref, f32[256,512]{1,0:T(8,128)S(1)} %get-tuple-element.12.c_ref, f32[256,512]{1,0:T(8,128)S(1)} %get-tuple-element.13.d_ref, ...), custom_call_target="tpu_custom_call" | custom-call | tf_op jit(solution)/shard_map/pallas_call | solution.py:843
Async XLA Ops:
  0.6 0.8 copy-start

commit v5 on v4

--- a/solution.py
+++ b/solution.py
@@ -144,88 +144,85 @@
 ORDER = (1, 7, 2, 6, 3, 5, 4)
 
 
-def gather(at, send, recv, before=None, hooks=()):
-    _, core, x, z = place()
-
-    def slab(xx, zz):
-        return at(xx % NX, (zz + 2 * NZ) % NZ)
-
-    def along_z(dx, dist):
+class Gather:
+    def __init__(self, at, send, recv):
+        _, self.core, self.x, self.z = place()
+        self.at, self.send, self.recv = at, send, recv
+
+    def slab(self, xx, zz):
+        return self.at(xx % NX, (zz + 2 * NZ) % NZ)
+
+    def copy(self, piece, dx, dist, x, z):
+        return remote(piece, piece, self.send.at[dx, dist], self.recv.at[dx, dist], {"pcol": x % NX * NZ + (z + NZ) % NZ})
+
+    def along_z(self, dx, dist):
         step = 1 if dist <= NZ // 2 else -1
-        piece = slab(x + dx, z + step - dist)
-        return remote(piece, piece, send.at[dx, dist], recv.at[dx, dist], {"pcol": x * NZ + (z + step + NZ) % NZ})
-
-    def along_x(dx, dist):
-        piece = slab(x, z - dist)
-        return remote(piece, piece, send.at[dx, dist], recv.at[dx, dist], {"pcol": (x + NX - dx) % NX * NZ + z})
-
-    def arrived(dx, dist):
-        piece = slab(x + dx, z - dist)
-        remote(piece, piece, send.at[dx, dist], recv.at[dx, dist], {"pcol": x * NZ + (z + 1) % NZ}).wait_recv()
-
-    def passed_on(dx, dist):
+        return self.copy(self.slab(self.x + dx, self.z + step - dist), dx, dist, self.x, self.z + step)
+
+    def along_x(self, dx, dist):
+        return self.copy(self.slab(self.x, self.z - dist), dx, dist, self.x + NX - dx, self.z)
+
+    def arrived(self, dx, dist):
+        self.copy(self.slab(self.x + dx, self.z - dist), dx, dist, self.x, self.z + 1).wait_recv()
+
+    def passed_on(self, dx, dist):
         if dist < NZ // 2:
-            along_z(dx, dist + 1).start()
+            self.along_z(dx, dist + 1).start()
         elif dist > NZ // 2 + 1:
-            along_z(dx, dist - 1).start()
-
-    @pl.when(core == 0)
-    def _():
-        along_z(0, 1).start()
-        along_z(0, NZ - 1).start()
-        for dx in range(1, NX):
-            along_x(dx, 0).start()
-
-    @pl.when(core == 1)
-    def _():
-        for dx in range(1, NX):
-            along_x(dx, 0).start()
-        along_z(0, 1).start()
-        along_z(0, NZ - 1).start()
-
-    if before:
-        before()
-
-    @pl.when(core == 1)
-    def _():
-        for dx in range(1, NX):
-            arrived(dx, 0)
-            along_z(dx, 1).start()
-            along_z(dx, NZ - 1).start()
-
-    for i, dist in enumerate(ORDER):
-
-        @pl.when(core == 0)
-        def _():
-            arrived(0, dist)
-            passed_on(0, dist)
+            self.along_z(dx, dist - 1).start()
+
+    def start(self):
+        @pl.when(self.core == 0)
+        def _():
+            self.along_z(0, 1).start()
+            self.along_z(0, NZ - 1).start()
             for dx in range(1, NX):
-                along_x(dx, dist).start()
+                self.along_x(dx, 0).start()
+
+        @pl.when(self.core == 1)
+        def _():
             for dx in range(1, NX):
-                arrived(dx, ORDER[i - 1] if i else 0)
-
-        @pl.when(core == 1)
+                self.along_x(dx, 0).start()
+            self.along_z(0, 1).start()
+            self.along_z(0, NZ - 1).start()
+
+    def enter(self):
+        @pl.when(self.core == 1)
+        def _():
+            for dx in range(1, NX):
+                self.arrived(dx, 0)
+                self.along_z(dx, 1).start()
+                self.along_z(dx, NZ - 1).start()
+
+    def step(self, i):
+        dist = ORDER[i]
+
+        @pl.when(self.core == 0)
+        def _():
+            self.arrived(0, dist)
+            self.passed_on(0, dist)
+            for dx in range(1, NX):
+                self.along_x(dx, dist).start()
+            for dx in range(1, NX):
+                self.arrived(dx, ORDER[i - 1] if i else 0)
+
+        @pl.when(self.core == 1)
         def _():
             for dx in range(NX):
-                arrived(dx, dist)
-                passed_on(dx, dist)
-
-        if i < len(hooks):
-            hooks[i]()
-
-    @pl.when(core == 0)
-    def _():
-        for dx in range(1, NX):
-            arrived(dx, ORDER[-1])
-
-    def flush():
+                self.arrived(dx, dist)
+                self.passed_on(dx, dist)
+
+    def end(self):
+        @pl.when(self.core == 0)
+        def _():
+            for dx in range(1, NX):
+                self.arrived(dx, ORDER[-1])
+
+    def flush(self):
         for dx in range(NX):
             for dist in range(NZ):
                 if dx or dist:
-                    piece = slab(x, z)
-                    remote(piece, piece, send.at[dx, dist], recv.at[dx, dist], {"pcol": x * NZ + (z + 1) % NZ}).wait_send()
-
-    return flush
+                    self.copy(self.slab(self.x, self.z), dx, dist, self.x, self.z + 1).wait_send()
 
 
 class Broadcast:
@@ -406,19 +403,22 @@
 def main_kernel(
     slab_ref,
     a_ref,
-    pt_ref,
-    out_ref,
+    pt_out,
+    ap_out,
+    ae_out,
     c_ref,
     d_ref,
+    e_ref,
     b_ref,
     l_ref,
+    pt_ref,
+    apr,
+    aer,
     a_buf,
     a_hi,
     a_lo,
     ae,
     aet,
-    ae64,
-    ap64,
     gram,
     gfull,
     gparts,
@@ -455,6 +455,8 @@
     frecv,
     ksend,
     krecv,
+    rsend,
+    rrecv,
     send,
     recv,
     xsend,
@@ -468,7 +470,7 @@
 ):
     y, core, x, z = place()
     prow, pcol = y * 2 + core, x * NZ + z
-    nb = out_ref.shape[1]
+    nb = apr.shape[1]
     cols = ae.shape[1]
     rows = cols // 8
     q = nb // 8
@@ -476,6 +478,9 @@
 
     load = pltpu.make_async_copy(a_ref, a_buf, acopy.at[0])
     load.start()
+    own_slab = pt_ref.at[x, pl.ds(pl.multiple_of(z * 8, 8), 8)]
+    take = pltpu.make_async_copy(slab_ref, own_slab, acopy.at[1])
+    take.start()
 
     to_row, to_col = pcol // 4, pcol % 4 * 8 + core * NY + y
     source_col, j = prow * 4 + pcol // 8, pcol % 8
@@ -502,9 +507,15 @@
     def _():
         greet({"prow": 0, "pcol": source_col})
 
-    pt_ref[x, pl.ds(pl.multiple_of(z * 8, 8), 8), :] = slab_ref[...]
     extra = jnp.where(moves, 1, 0) + jnp.where(prow == 0, 8, 0) - jnp.where(corner, 1, 0)
     pl.semaphore_wait(barrier, len(peers) + extra)
+    take.wait()
+
+    def slab_rows(c):
+        return pl.ds(pl.multiple_of(c * rows, rows), rows)
+
+    def slabs(ref):
+        return lambda xx, zz: ref.at[slab_rows(xx * NZ + zz)]
 
     top = Broadcast(0, 0, a_ref.at[pl.ds(0, nb)], ae, esend, erecv)
     window = pl.ds(pl.multiple_of(pcol % 4 * cols, cols), cols)
@@ -513,7 +524,8 @@
 
     def top_piece(k):
         peer = {"prow": pcol // 4, "pcol": pcol % 4 * 8 + k}
-        return remote(aet.at[pl.ds(k * rows, rows)], ae64, ksend.at[k], krecv.at[0], peer)
+        dst = aer.at[slab_rows(pcol % 4 * 8 + k)]
+        return remote(aet.at[pl.ds(k * rows, rows)], dst, ksend.at[k], krecv.at[0], peer)
 
     def take_a():
         load.wait()
@@ -531,15 +543,31 @@
 
         @pl.when(corner)
         def _():
-            ae64[...] = aet[0:rows, :]
-
-    panel_flush = gather(
-        lambda xx, zz: pt_ref.at[xx, pl.ds(pl.multiple_of(zz * 8, 8), 8)],
-        panel_send,
-        panel_recv,
-        top.start,
-        (lambda: None, take_a),
+            aer[0:rows, :] = aet[0:rows, :]
+
+    pgather = Gather(
+        lambda xx, zz: pt_ref.at[xx, pl.ds(pl.multiple_of(zz * 8, 8), 8)], panel_send, panel_recv
     )
+    egather = Gather(slabs(aer), rsend, rrecv)
+    agather = Gather(slabs(apr), send, recv)
+    pgather.start()
+    top.start()
+    pgather.enter()
+    for i in range(7):
+        pgather.step(i)
+        if i == 1:
+            take_a()
+    pgather.end()
+    keep_p = pltpu.make_async_copy(pt_ref, pt_out, acopy.at[2])
+    keep_a = pltpu.make_async_copy(apr, ap_out, acopy.at[3])
+    keep_e = pltpu.make_async_copy(aer, ae_out, acopy.at[4])
+    keep_p.start()
+
+    @pl.when(jnp.logical_not(corner))
+    def _():
+        top_piece(0).wait_recv()
+
+    egather.start()
     panel = pt_ref[...].reshape(nb, wide)
     gram[...] = mm(panel, panel, NT)
 
@@ -549,15 +577,17 @@
     gsum.start()
     aps[...] = mm3(split(panel), (a_hi[...], a_lo[...])).T
     asum.exchange()
+    egather.enter()
     gfull[gsum.rows(0), :] = gsum.total()
     gsum.share()
+    egather.step(0)
     asum.quarters()
     head.start()
     gsum.finish()
 
-    swap = remote(apt.at[asum.own], ap64, fsend.at[0], frecv.at[0], {"prow": to_row, "pcol": to_col})
-
-    def hand_on():
+    swap = remote(apt.at[asum.own], apr.at[slab_rows(to_col)], fsend.at[0], frecv.at[0], {"prow": to_row, "pcol": to_col})
+
+    def chol_first():
         asum.total()
 
         @pl.when(moves)
@@ -566,25 +596,33 @@
 
         @pl.when(stays)
         def _():
-            ap64[...] = apt[asum.own, :]
-
-    def relay():
+            apr[slab_rows(pcol), :] = apt[asum.own, :]
+
+        egather.step(1)
+
+    def chol_second():
+        head.near()
+        egather.step(2)
+        egather.step(3)
+        asum.spread()
+
+    def chol_third():
+        @pl.when(moves)
+        def _():
+            swap.wait_recv()
+
+        agather.start()
+        top.near()
+        egather.step(4)
+
+    def chol_fourth():
         head.far()
-        top.near()
-
-    stages = iter([hand_on, head.near, relay, lambda: None])
+        egather.step(5)
+        agather.enter()
+
+    stages = iter([chol_first, chol_second, chol_third, chol_fourth])
     linv = lower_inverse(gfull[...], lambda: next(stages)())
     linv_s[...] = linv
-
-    @pl.when(moves)
-    def _():
-        swap.wait_recv()
-
-    @pl.when(jnp.logical_not(corner))
-    def _():
-        top_piece(0).wait_recv()
-
-    out_ref[pl.ds(pl.multiple_of(pcol * rows, rows), rows), :] = mm(ap64[...], linv, NT) - ae64[...]
 
     def along_x(src, dst, sends, recvs, dx):
         return remote(src, dst, sends.at[dx], recvs.at[dx], {"pcol": (x + dx) % NX * NZ + z})
@@ -599,7 +637,7 @@
         row, lane = iota((nb, lanes), 0), iota((nb, lanes), 1)
         v = mm(linv_s[...], p) - (row == lane + block + prow * wide).astype(F32)
         v = jnp.where(lane // rows == pcol % 2, v, 0.0)
-        av = out_ref[pl.ds(pl.multiple_of(pcol * rows, rows), rows), :]
+        av = mm(apr[slab_rows(pcol), :], linv_s[...], NT) - aer[slab_rows(pcol), :]
         mpart[...] = mm(v, jnp.concatenate([av, av], 0))
         msum.start()
 
@@ -657,37 +695,31 @@
         for lo, hi, side in sides:
             t_s[lo, hi] = side
 
-    def before():
-        asum.spread()
-        part.start()
-        m_scatter()
-        head.finish()
-
-    def first():
-        factor_first()
-        top.far()
-
-    def second():
-        m_x()
-        asum.forward()
-
-    def fourth():
-        m_z()
-        part.near()
-
-    def fifth():
-        merge(BASE)
-        merge(2 * BASE)
-        part.far()
-
-    flush = gather(
-        lambda xx, zz: out_ref.at[pl.ds(pl.multiple_of((xx * NZ + zz) * rows, rows), rows)],
-        send,
-        recv,
-        before,
-        (first, second, factor_second, fourth, fifth, m_back, m_share),
-    )
-
+    m_scatter()
+    part.start()
+    egather.step(6)
+    agather.step(0)
+    egather.end()
+    keep_e.start()
+    head.finish()
+    factor_first()
+    asum.forward()
+    top.far()
+    agather.step(1)
+    m_x()
+    agather.step(2)
+    factor_second()
+    agather.step(3)
+    m_z()
+    part.near()
+    merge(BASE)
+    agather.step(4)
+    merge(2 * BASE)
+    m_back()
+    part.far()
+    agather.step(5)
+    m_share()
+    agather.step(6)
     asum.finish()
     top.finish()
     part.finish()
@@ -695,7 +727,11 @@
     e = (iota((nb, cols), 0) == iota((nb, cols), 1)) & (pcol == 0)
     vct = mm(linv, pct[...].reshape(nb, cols)) - e.astype(F32)
     xc = mm(t, mm(linv, apt[...], NT) - ae[...], TN)
-    d_ref[...] = mm(t, vct)
+    d = mm(t, vct)
+    e_ref[...] = d
+    d_ref[...] = mm(linv, d, TN)
+    agather.end()
+    keep_a.start()
     msum.finish()
     k = mm(t, mm(mraw[...], t), TN)
     b = xc - mm(0.5 * (k + k.T), vct)
@@ -705,10 +741,16 @@
     kt = mm(sel, k, NT)
     l_ref[0:8, :] = kt
     l_ref[8:16, :] = mm(kt, linv)
-    l_ref[16:24, :] = mm(sel, t, NT)
-
-    flush()
-    panel_flush()
+    ts = mm(sel, t, NT)
+    l_ref[16:24, :] = mm(ts, linv)
+    l_ref[24:32, :] = ts
+
+    pgather.flush()
+    egather.flush()
+    agather.flush()
+    keep_p.wait()
+    keep_e.wait()
+    keep_a.wait()
     gsum.flush()
     asum.flush()
     msum.flush()
@@ -745,19 +787,20 @@
     return jax.ShapeDtypeStruct(dims, F32)
 
 
-def update_kernel(a_ref, pt_ref, av_ref, c_ref, d_ref, b_ref, l_ref, o_ref, w_ref, ch, cl, dh, dl):
+def update_kernel(a_ref, pt_ref, ap_ref, ae_ref, c_ref, d_ref, e_ref, b_ref, l_ref, o_ref, w_ref, ch, cl, dh, dl, eh, el):
     step = pl.program_id(0)
 
     @pl.when(step == 0)
     def _():
         ch[...], cl[...] = split(c_ref[...])
         dh[...], dl[...] = split(d_ref[...])
-
-    p, v = pt_ref[...], av_ref[...]
-    ps, vs = split(p), split(v)
-    both = mm3(ps, (ch[...], cl[...]), TN) + mm3(vs, (dh[...], dl[...]))
+        eh[...], el[...] = split(-e_ref[...])
+
+    ps, vs, es = split(pt_ref[...]), split(ap_ref[...]), split(ae_ref[...])
+    both = mm3(ps, (ch[...], cl[...]), TN) + mm3(vs, (dh[...], dl[...])) + mm3(es, (eh[...], el[...]))
     o_ref[...] = a_ref[...] - both
-    w_ref[...] = mm3(split(l_ref[16:24, :]), vs, NT) - 0.5 * mm3(split(l_ref[8:16, :]), ps)
+    w = mm3(split(l_ref[16:24, :]), vs, NT) - mm3(split(l_ref[24:32, :]), es, NT)
+    w_ref[...] = w - 0.5 * mm3(split(l_ref[8:16, :]), ps)
 
     @pl.when((lax.axis_index("prow") == 0) & (step == 0))
     def _():
@@ -775,19 +818,20 @@
     buf = lambda *dims: pltpu.VMEM(dims, F32)
 
     q = nb // 8
-    pt, av, c, d, b, l = pl.pallas_call(
+    pt, ap, ae, c, d, e, b, l = pl.pallas_call(
         main_kernel,
-        out_shape=(shape(NX, nb // NX, rows), shape(rows, nb)) + (shape(nb, cols),) * 3 + (shape(24, nb),),
-        in_specs=[VMEM, ANY],
-        out_specs=(VMEM,) * 6,
+        out_shape=(shape(NX, nb // NX, rows),) + (shape(rows, nb),) * 2 + (shape(nb, cols),) * 4 + (shape(32, nb),),
+        in_specs=[ANY, ANY],
+        out_specs=(ANY,) * 3 + (VMEM,) * 5,
         scratch_shapes=[
+            buf(NX, nb // NX, rows),
+            buf(rows, nb),
+            buf(rows, nb),
             buf(rows, cols),
             pltpu.VMEM((rows, cols), jnp.bfloat16),
             pltpu.VMEM((rows, cols), jnp.bfloat16),
             buf(nb, cols),
             buf(cols, nb),
-            buf(cols // 8, nb),
-            buf(cols // 8, nb),
             buf(nb, nb),
             buf(nb, nb),
             buf(8, q, nb),
@@ -807,7 +851,7 @@
             buf(NZ, 8, nb),
             buf(8, nb),
             buf(nb, nb),
-            dma((1,)),
+            dma((5,)),
             dma((NX, NZ)),
             dma((NX, NZ)),
             dma((4,)),
@@ -826,6 +870,8 @@
             dma((1,)),
             dma((NX, NZ)),
             dma((NX, NZ)),
+            dma((NX, NZ)),
+            dma((NX, NZ)),
             dma((NX,)),
             dma((NX,)),
             dma((NZ,)),
@@ -848,15 +894,17 @@
             pl.BlockSpec((tile, cols), lambda i: (i, 0)),
             pl.BlockSpec((nb, tile), lambda i: (0, i)),
             pl.BlockSpec((tile, nb), lambda i: (i, 0)),
+            pl.BlockSpec((tile, nb), lambda i: (i, 0)),
             whole(nb, cols),
             whole(nb, cols),
             whole(nb, cols),
-            whole(24, nb),
+            whole(nb, cols),
+            whole(32, nb),
         ],
         out_specs=(pl.BlockSpec((tile, cols), lambda i: (i, 0)), pl.BlockSpec((nc, tile), lambda i: (0, i))),
-        scratch_shapes=[pltpu.VMEM((nb, cols), jnp.bfloat16)] * 4,
+        scratch_shapes=[pltpu.VMEM((nb, cols), jnp.bfloat16)] * 6,
         compiler_params=plain(dimension_semantics=("arbitrary",)),
-    )(trailing, pt.reshape(nb, rows), av, c, d, b, l)
+    )(trailing, pt.reshape(nb, rows), ap, ae, c, d, e, b, l)
     return updated, wt.T
 
 

time: 122 us -> 131 us (1.074); the launches traced: 122 us -> 129 us
  Pallas kernels: 120 us -> 128 us
    pallas_call x1, Pallas kernels: 112 us -> 117 us  [shards(): pl.pallas_call(main_kernel, out_shape=(shape(NX, nb // NX, rows),) + (sha...]
    pallas_call x1, Pallas kernels: 7.9 us -> 10.4 us  [shards(): pl.pallas_call(update_kernel, grid=(rows // tile,), out_shape=(shape(rows...]
where the time goes in v5:
time: 131 us; the launch traced here: 129 us
  Pallas kernels  128 us (98%)
    pallas_call x1, Pallas kernels, shards(): pl.pallas_call(main_kernel, out_shape=(shape(NX, nb // NX, rows),) + (sha...  117 us
    pallas_call x1, Pallas kernels, shards(): pl.pallas_call(update_kernel, grid=(rows // tile,), out_shape=(shape(rows...  10.4 us

profile of v5, /device:TPU:1, one launch (start us, length us, event | category | flops | bytes accessed | tf_op | source)
XLA Modules:
  0.0 129.2 jit_solution(7963867726620085491)
XLA Ops:
  0.6 0.0 copy-start
  0.6 0.8 copy-done
  1.5 117.4 %shard_map.41 = (f32[4,64,2048]{2,1,0:T(8,128)S(1)}, f32[2048,256]{1,0:T(8,128)}, f32[2048,256]{1,0:T(8,128)}, f32[256,512]{1,0:T(8,128)S(1)}, f32[256,512]{1,0:...) custom-call(f32[8,2048]{1,0:T(8,128)S(1)} %bitcast.4, f32[2048,512]{1,0:T(8,128)} %a_ref.3), custom_call_target="tpu_custom_call" | custom-call | tf_op jit(solution)/shard_map/pallas_call | solution.py:821
  118.9 10.4 %shard_map.42 = (f32[2048,512]{1,0:T(8,128)}, f32[8,2048]{1,0:T(8,128)}) custom-call(f32[2048,512]{1,0:T(8,128)} %a_ref.3, f32[256,2048]{1,0:T(8,128)S(1)} %bitcast.3, f32[2048,256]{1,0:T(8,128)} %get-tuple-element.13.ap_ref, f32[2048,256]{1,0:T(8,128)} %get-tuple-element.14.ae_ref, f32[256,512]{1,0:T(8,128)S(1)} %get-tuple-element.15.c_ref, ...), custom_call_target="tpu_custom_call" | custom-call | tf_op jit(solution)/shard_map/pallas_call | solution.py:889
Async XLA Ops:
  0.6 0.8 copy-start

commit v6 on v4

--- a/solution.py
+++ b/solution.py
@@ -406,12 +406,13 @@
 def main_kernel(
     slab_ref,
     a_ref,
-    pt_ref,
+    pt_out,
     out_ref,
     c_ref,
     d_ref,
     b_ref,
     l_ref,
+    pt_ref,
     a_buf,
     a_hi,
     a_lo,
@@ -476,6 +477,8 @@
 
     load = pltpu.make_async_copy(a_ref, a_buf, acopy.at[0])
     load.start()
+    take = pltpu.make_async_copy(slab_ref, pt_ref.at[x, pl.ds(pl.multiple_of(z * 8, 8), 8)], acopy.at[1])
+    take.start()
 
     to_row, to_col = pcol // 4, pcol % 4 * 8 + core * NY + y
     source_col, j = prow * 4 + pcol // 8, pcol % 8
@@ -502,9 +505,9 @@
     def _():
         greet({"prow": 0, "pcol": source_col})
 
-    pt_ref[x, pl.ds(pl.multiple_of(z * 8, 8), 8), :] = slab_ref[...]
     extra = jnp.where(moves, 1, 0) + jnp.where(prow == 0, 8, 0) - jnp.where(corner, 1, 0)
     pl.semaphore_wait(barrier, len(peers) + extra)
+    take.wait()
 
     top = Broadcast(0, 0, a_ref.at[pl.ds(0, nb)], ae, esend, erecv)
     window = pl.ds(pl.multiple_of(pcol % 4 * cols, cols), cols)
@@ -537,9 +540,11 @@
         lambda xx, zz: pt_ref.at[xx, pl.ds(pl.multiple_of(zz * 8, 8), 8)],
         panel_send,
         panel_recv,
-        top.start,
+        None,
         (lambda: None, take_a),
     )
+    keep = pltpu.make_async_copy(pt_ref, pt_out, acopy.at[2])
+    keep.start()
     panel = pt_ref[...].reshape(nb, wide)
     gram[...] = mm(panel, panel, NT)
 
@@ -554,6 +559,7 @@
     asum.quarters()
     head.start()
     gsum.finish()
+    top.start()
 
     swap = remote(apt.at[asum.own], ap64, fsend.at[0], frecv.at[0], {"prow": to_row, "pcol": to_col})
 
@@ -569,10 +575,10 @@
             ap64[...] = apt[asum.own, :]
 
     def relay():
-        head.far()
         top.near()
-
-    stages = iter([hand_on, head.near, relay, lambda: None])
+        part.start()
+
+    stages = iter([hand_on, head.near, head.far, relay])
     linv = lower_inverse(gfull[...], lambda: next(stages)())
     linv_s[...] = linv
 
@@ -659,7 +665,6 @@
 
     def before():
         asum.spread()
-        part.start()
         m_scatter()
         head.finish()
 
@@ -671,13 +676,19 @@
         m_x()
         asum.forward()
 
+    def third():
+        factor_second()
+        part.near()
+
     def fourth():
         m_z()
-        part.near()
 
     def fifth():
         merge(BASE)
         merge(2 * BASE)
+
+    def sixth():
+        m_back()
         part.far()
 
     flush = gather(
@@ -685,7 +696,7 @@
         send,
         recv,
         before,
-        (first, second, factor_second, fourth, fifth, m_back, m_share),
+        (first, second, third, fourth, fifth, sixth, m_share),
     )
 
     asum.finish()
@@ -693,14 +704,16 @@
     part.finish()
     linv, t = linv_s[...], t_s[...]
     e = (iota((nb, cols), 0) == iota((nb, cols), 1)) & (pcol == 0)
-    vct = mm(linv, pct[...].reshape(nb, cols)) - e.astype(F32)
-    xc = mm(t, mm(linv, apt[...], NT) - ae[...], TN)
-    d_ref[...] = mm(t, vct)
+    ls, ts = split(linv), split(t)
+    vct = mm3(ls, split(pct[...].reshape(nb, cols))) - e.astype(F32)
+    vs = split(vct)
+    xc = mm3(ts, split(mm3(ls, split(apt[...]), NT) - ae[...]), TN)
+    d_ref[...] = mm3(ts, vs)
     msum.finish()
-    k = mm(t, mm(mraw[...], t), TN)
-    b = xc - mm(0.5 * (k + k.T), vct)
+    k = mm3(ts, split(mm3(split(mraw[...]), ts)), TN)
+    b = xc - mm3(split(0.5 * (k + k.T)), vs)
     b_ref[...] = b
-    c_ref[...] = mm(linv, b, TN)
+    c_ref[...] = mm3(ls, split(b), TN)
     sel = (iota((8, nb), 1) == iota((8, nb), 0) + 8 * pcol).astype(F32)
     kt = mm(sel, k, NT)
     l_ref[0:8, :] = kt
@@ -709,6 +722,7 @@
 
     flush()
     panel_flush()
+    keep.wait()
     gsum.flush()
     asum.flush()
     msum.flush()
@@ -778,9 +792,10 @@
     pt, av, c, d, b, l = pl.pallas_call(
         main_kernel,
         out_shape=(shape(NX, nb // NX, rows), shape(rows, nb)) + (shape(nb, cols),) * 3 + (shape(24, nb),),
-        in_specs=[VMEM, ANY],
-        out_specs=(VMEM,) * 6,
+        in_specs=[ANY, ANY],
+        out_specs=(ANY,) + (VMEM,) * 5,
         scratch_shapes=[
+            buf(NX, nb // NX, rows),
             buf(rows, cols),
             pltpu.VMEM((rows, cols), jnp.bfloat16),
             pltpu.VMEM((rows, cols), jnp.bfloat16),
@@ -807,7 +822,7 @@
             buf(NZ, 8, nb),
             buf(8, nb),
             buf(nb, nb),
-            dma((1,)),
+            dma((3,)),
             dma((NX, NZ)),
             dma((NX, NZ)),
             dma((4,)),

time: 122 us -> 125 us (1.025)
  Pallas kernels: 120 us -> 123 us
    pallas_call x1, Pallas kernels: 112 us -> 116 us  [shards(): pl.pallas_call(main_kernel, out_shape=(shape(NX, nb // NX, rows), shape(r...]
where the time goes in v6:
time: 125 us
  Pallas kernels  123 us (98%)
    pallas_call x1, Pallas kernels, shards(): pl.pallas_call(main_kernel, out_shape=(shape(NX, nb // NX, rows), shape(r...  116 us
    pallas_call x1, Pallas kernels, shards(): pl.pallas_call(update_kernel, grid=(rows // tile,), out_shape=(shape(rows...  7.9 us

profile of v6, /device:TPU:1, one launch (start us, length us, event | category | flops | bytes accessed | tf_op | source)
XLA Modules:
  0.0 124.9 jit_solution(188921390570646309)
XLA Ops:
  0.6 0.0 copy-start
  0.6 0.8 copy-done
  1.5 115.5 %shard_map.41 = (f32[4,64,2048]{2,1,0:T(8,128)S(1)}, f32[2048,256]{1,0:T(8,128)S(1)}, f32[256,512]{1,0:T(8,128)S(1)}, f32[256,512]{1,0:T(8,128)S(1)}, f32[256,512]{1,0:T(8,128)S(1)}, /*index=5*/f32[24,256]{1,0:T(8,128)S(1)}) custom-call(f32[8,2048]{1,0:T(8,128)S(1)} %bitcast.4, f32[2048,512]{1,0:T(8,128)} %a_ref.3), custom_call_target="tpu_custom_call" | custom-call | tf_op jit(solution)/shard_map/pallas_call | solution.py:792
  117.0 7.9 %shard_map.42 = (f32[2048,512]{1,0:T(8,128)}, f32[8,2048]{1,0:T(8,128)}) custom-call(f32[2048,512]{1,0:T(8,128)} %a_ref.3, f32[256,2048]{1,0:T(8,128)S(1)} %bitcast.3, f32[2048,256]{1,0:T(8,128)S(1)} %get-tuple-element.11.av_ref, f32[256,512]{1,0:T(8,128)S(1)} %get-tuple-element.12.c_ref, f32[256,512]{1,0:T(8,128)S(1)} %get-tuple-element.13.d_ref, ...), custom_call_target="tpu_custom_call" | custom-call | tf_op jit(solution)/shard_map/pallas_call | solution.py:858
Async XLA Ops:
  0.6 0.8 copy-start

commit v7 on v6

--- a/solution.py
+++ b/solution.py
@@ -536,12 +536,16 @@
         def _():
             ae64[...] = aet[0:rows, :]
 
+    def begin():
+        top.start()
+        take_a()
+
     panel_flush = gather(
         lambda xx, zz: pt_ref.at[xx, pl.ds(pl.multiple_of(zz * 8, 8), 8)],
         panel_send,
         panel_recv,
-        None,
-        (lambda: None, take_a),
+        begin,
+        (),
     )
     keep = pltpu.make_async_copy(pt_ref, pt_out, acopy.at[2])
     keep.start()
@@ -559,7 +563,6 @@
     asum.quarters()
     head.start()
     gsum.finish()
-    top.start()
 
     swap = remote(apt.at[asum.own], ap64, fsend.at[0], frecv.at[0], {"prow": to_row, "pcol": to_col})
 
@@ -575,10 +578,10 @@
             ap64[...] = apt[asum.own, :]
 
     def relay():
+        head.far()
         top.near()
-        part.start()
-
-    stages = iter([hand_on, head.near, head.far, relay])
+
+    stages = iter([hand_on, head.near, relay, lambda: None])
     linv = lower_inverse(gfull[...], lambda: next(stages)())
     linv_s[...] = linv
 
@@ -665,11 +668,15 @@
 
     def before():
         asum.spread()
+        part.start()
         m_scatter()
         head.finish()
+        factor_first()
+        factor_second()
+        merge(BASE)
+        merge(2 * BASE)
 
     def first():
-        factor_first()
         top.far()
 
     def second():
@@ -677,15 +684,14 @@
         asum.forward()
 
     def third():
-        factor_second()
-        part.near()
+        pass
 
     def fourth():
         m_z()
+        part.near()
 
     def fifth():
-        merge(BASE)
-        merge(2 * BASE)
+        pass
 
     def sixth():
         m_back()

time: 125 us -> 117 us (0.936)
  Pallas kernels: 123 us -> 115 us
    pallas_call x1, Pallas kernels: 116 us -> 107 us  [shards(): pl.pallas_call(main_kernel, out_shape=(shape(NX, nb // NX, rows), shape(r...]
where the time goes in v7:
time: 117 us
  Pallas kernels  115 us (98%)
    pallas_call x1, Pallas kernels, shards(): pl.pallas_call(main_kernel, out_shape=(shape(NX, nb // NX, rows), shape(r...  107 us
    pallas_call x1, Pallas kernels, shards(): pl.pallas_call(update_kernel, grid=(rows // tile,), out_shape=(shape(rows...  7.9 us

profile of v7, /device:TPU:1, one launch (start us, length us, event | category | flops | bytes accessed | tf_op | source)
XLA Modules:
  0.0 116.6 jit_solution(7967128372272310907)
XLA Ops:
  0.6 0.0 copy-start
  0.6 0.8 copy-done
  1.5 107.2 %shard_map.41 = (f32[4,64,2048]{2,1,0:T(8,128)S(1)}, f32[2048,256]{1,0:T(8,128)S(1)}, f32[256,512]{1,0:T(8,128)S(1)}, f32[256,512]{1,0:T(8,128)S(1)}, f32[256,512]{1,0:T(8,128)S(1)}, /*index=5*/f32[24,256]{1,0:T(8,128)S(1)}) custom-call(f32[8,2048]{1,0:T(8,128)S(1)} %bitcast.4, f32[2048,512]{1,0:T(8,128)} %a_ref.3), custom_call_target="tpu_custom_call" | custom-call | tf_op jit(solution)/shard_map/pallas_call | solution.py:798
  108.7 7.9 %shard_map.42 = (f32[2048,512]{1,0:T(8,128)}, f32[8,2048]{1,0:T(8,128)}) custom-call(f32[2048,512]{1,0:T(8,128)} %a_ref.3, f32[256,2048]{1,0:T(8,128)S(1)} %bitcast.3, f32[2048,256]{1,0:T(8,128)S(1)} %get-tuple-element.11.av_ref, f32[256,512]{1,0:T(8,128)S(1)} %get-tuple-element.12.c_ref, f32[256,512]{1,0:T(8,128)S(1)} %get-tuple-element.13.d_ref, ...), custom_call_target="tpu_custom_call" | custom-call | tf_op jit(solution)/shard_map/pallas_call | solution.py:864
Async XLA Ops:
  0.6 0.8 copy-start

commit v8 on v7

--- a/solution.py
+++ b/solution.py
@@ -677,54 +677,54 @@
         merge(2 * BASE)
 
     def first():
+        m_x()
         top.far()
 
     def second():
-        m_x()
         asum.forward()
-
-    def third():
-        pass
+        m_z()
 
     def fourth():
-        m_z()
+        m_back()
         part.near()
 
     def fifth():
-        pass
+        m_share()
 
     def sixth():
-        m_back()
         part.far()
-
+        asum.finish()
+        top.finish()
+
+    def last():
+        part.finish()
+        matrices()
+
+    def matrices():
+        linv, t = linv_s[...], t_s[...]
+        e = (iota((nb, cols), 0) == iota((nb, cols), 1)) & (pcol == 0)
+        ls, ts = split(linv), split(t)
+        vct = mm3(ls, split(pct[...].reshape(nb, cols))) - e.astype(F32)
+        vs = split(vct)
+        xc = mm3(ts, split(mm3(ls, split(apt[...]), NT) - ae[...]), TN)
+        d_ref[...] = mm3(ts, vs)
+        msum.finish()
+        k = mm3(ts, split(mm3(split(mraw[...]), ts)), TN)
+        b = xc - mm3(split(0.5 * (k + k.T)), vs)
+        b_ref[...] = b
+        c_ref[...] = mm3(ls, split(b), TN)
+        sel = (iota((8, nb), 1) == iota((8, nb), 0) + 8 * pcol).astype(F32)
+        kt = mm(sel, k, NT)
+        l_ref[0:8, :] = kt
+        l_ref[8:16, :] = mm(kt, linv)
+        l_ref[16:24, :] = mm(sel, t, NT)
     flush = gather(
         lambda xx, zz: out_ref.at[pl.ds(pl.multiple_of((xx * NZ + zz) * rows, rows), rows)],
         send,
         recv,
         before,
-        (first, second, third, fourth, fifth, sixth, m_share),
+        (first, second, lambda: None, fourth, fifth, sixth, last),
     )
-
-    asum.finish()
-    top.finish()
-    part.finish()
-    linv, t = linv_s[...], t_s[...]
-    e = (iota((nb, cols), 0) == iota((nb, cols), 1)) & (pcol == 0)
-    ls, ts = split(linv), split(t)
-    vct = mm3(ls, split(pct[...].reshape(nb, cols))) - e.astype(F32)
-    vs = split(vct)
-    xc = mm3(ts, split(mm3(ls, split(apt[...]), NT) - ae[...]), TN)
-    d_ref[...] = mm3(ts, vs)
-    msum.finish()
-    k = mm3(ts, split(mm3(split(mraw[...]), ts)), TN)
-    b = xc - mm3(split(0.5 * (k + k.T)), vs)
-    b_ref[...] = b
-    c_ref[...] = mm3(ls, split(b), TN)
-    sel = (iota((8, nb), 1) == iota((8, nb), 0) + 8 * pcol).astype(F32)
-    kt = mm(sel, k, NT)
-    l_ref[0:8, :] = kt
-    l_ref[8:16, :] = mm(kt, linv)
-    l_ref[16:24, :] = mm(sel, t, NT)
 
     flush()
     panel_flush()

time: 117 us -> 115 us (0.983)
  Pallas kernels: 115 us -> 112 us
    pallas_call x1, Pallas kernels: 107 us -> 104 us  [shards(): pl.pallas_call(main_kernel, out_shape=(shape(NX, nb // NX, rows), shape(r...]
where the time goes in v8:
time: 115 us; the launch traced here: 114 us
  Pallas kernels  112 us (97%)
    pallas_call x1, Pallas kernels, shards(): pl.pallas_call(main_kernel, out_shape=(shape(NX, nb // NX, rows), shape(r...  104 us
    pallas_call x1, Pallas kernels, shards(): pl.pallas_call(update_kernel, grid=(rows // tile,), out_shape=(shape(rows...  7.9 us

profile of v8, /device:TPU:1, one launch (start us, length us, event | category | flops | bytes accessed | tf_op | source)
XLA Modules:
  0.0 113.6 jit_solution(15579941943403069675)
XLA Ops:
  0.6 0.0 copy-start
  0.6 0.8 copy-done
  1.5 104.2 %shard_map.41 = (f32[4,64,2048]{2,1,0:T(8,128)S(1)}, f32[2048,256]{1,0:T(8,128)S(1)}, f32[256,512]{1,0:T(8,128)S(1)}, f32[256,512]{1,0:T(8,128)S(1)}, f32[256,512]{1,0:T(8,128)S(1)}, /*index=5*/f32[24,256]{1,0:T(8,128)S(1)}) custom-call(f32[8,2048]{1,0:T(8,128)S(1)} %bitcast.4, f32[2048,512]{1,0:T(8,128)} %a_ref.3), custom_call_target="tpu_custom_call" | custom-call | tf_op jit(solution)/shard_map/pallas_call | solution.py:798
  105.7 7.9 %shard_map.42 = (f32[2048,512]{1,0:T(8,128)}, f32[8,2048]{1,0:T(8,128)}) custom-call(f32[2048,512]{1,0:T(8,128)} %a_ref.3, f32[256,2048]{1,0:T(8,128)S(1)} %bitcast.3, f32[2048,256]{1,0:T(8,128)S(1)} %get-tuple-element.11.av_ref, f32[256,512]{1,0:T(8,128)S(1)} %get-tuple-element.12.c_ref, f32[256,512]{1,0:T(8,128)S(1)} %get-tuple-element.13.d_ref, ...), custom_call_target="tpu_custom_call" | custom-call | tf_op jit(solution)/shard_map/pallas_call | solution.py:864
Async XLA Ops:
  0.6 0.8 copy-start
